TPU v7x, 32 devices: a whole 2x2x4 slice. The times are simulated.
32 devices in a mesh: wide: 16 (over z, y, core), narrow: 2 (over x).
Axes of the slice: x: 2, y: 2, z: 4, core: 2. Of those that a mesh axis runs over, the one named last changes fastest.
Arguments:
- inputs: bfloat16 [2, 24576, 768], P(None, ('wide', 'narrow')), may hold values from -6 to 6
- coords: float32 [2, 2, 24576], P(None, None, ('wide', 'narrow')), may hold values from 0 to 1
- neighbours: int32 [2, 40, 24576], P(None, None, ('wide', 'narrow')), may hold values from 0 to 767, as said below
- counts: int32 [2, 24576], P(None, ('wide', 'narrow')), may hold values from 1 to 40, as said below
- doc_length: int32 [2, 32], P(None, ('wide', 'narrow')), may hold values from 384 to 768, as said below
- self_one: bfloat16 [768, 768], P(('wide', 'narrow')), may hold values from -0.21875 to 0.21875
- near_one: bfloat16 [768, 768], P(('wide', 'narrow')), may hold values from -0.4375 to 0.4375
- self_two: bfloat16 [768, 768], P(('wide', 'narrow')), may hold values from -0.21875 to 0.21875
- near_two: bfloat16 [768, 768], P(('wide', 'narrow')), may hold values from -0.4375 to 0.4375
- edge_proj: float32 [2, 768], replicated, may hold values from -4 to 4
- qkv_proj: bfloat16 [768, 2304], P(('wide', 'narrow')), may hold values from -0.21875 to 0.21875
- out_proj: bfloat16 [768, 768], P(('wide', 'narrow')), may hold values from -0.875 to 0.875
- up_proj: bfloat16 [768, 3072], P(('wide', 'narrow')), may hold values from -0.21875 to 0.21875
- down_proj: bfloat16 [3072, 768], P(('wide', 'narrow')), may hold values from -0.109375 to 0.109375
- norm_gains: float32 [3, 768], replicated, may hold values from 0.5 to 1.5
- norm_shifts: float32 [3, 768], replicated, may hold values from -1.5 to 1.5
- distance_rate: float32 [12], replicated, may hold values from 0.2 to 1
- order_rate: float32 [12], replicated, may hold values from -1 to 1
- cotangent: bfloat16 [2, 24576, 768], P(None, ('wide', 'narrow')), may hold values from -6 to 6
Outputs:
- outputs: bfloat16 [2, 24576, 768], P(None, ('wide', 'narrow'))
- input_grad: float32 [2, 24576, 768], P(None, ('wide', 'narrow'))
- grad_self_one: float32 [768, 768], P(('wide', 'narrow'))
- grad_near_one: float32 [768, 768], P(('wide', 'narrow'))
- grad_self_two: float32 [768, 768], P(('wide', 'narrow'))
- grad_near_two: float32 [768, 768], P(('wide', 'narrow'))
- grad_edge: float32 [2, 768], replicated
- grad_qkv: float32 [768, 2304], P(('wide', 'narrow'))
- grad_out: float32 [768, 768], P(('wide', 'narrow'))
- grad_up: float32 [768, 3072], P(('wide', 'narrow'))
- grad_down: float32 [3072, 768], P(('wide', 'narrow'))
- grad_gains: float32 [3, 768], replicated
- grad_shifts: float32 [3, 768], replicated
- grad_distance: float32 [12], replicated
- grad_order: float32 [12], replicated
Inputs may be any that keep to these rules, and one draw needn't show every extreme that they name: A token's neighbours are positions in its own row of 768 tokens, within 64 of its own position. `counts`: slots at or beyond a token's count are padding. `doc_length`: the rest of the row after the document is padding.
All inputs are finite; a program needn't handle non-finite values.
Results may differ from a plain program's by a relative error of at most 0.015.
Values may be sent and summed in bfloat16 or wider, within the bound.
A program may use at most 256 MiB of HBM per device.

v0:
```python
import jax
import jax.numpy as jnp
from jax import lax
from jax.sharding import PartitionSpec as P

RADIUS = 128


def dot_plain(left, right):
    return jnp.dot(left, right, preferred_element_type=jnp.float32)


def dot_left_t(left, right):
    return lax.dot_general(
        left, right, (((0,), (0,)), ((), ())), preferred_element_type=jnp.float32
    )


def dot_right_t(left, right):
    return lax.dot_general(
        left, right, (((1,), (1,)), ((), ())), preferred_element_type=jnp.float32
    )


def layer_norm(values, gain, shift):
    centre = values - jnp.mean(values, axis=-1, keepdims=True)
    spread = jnp.mean(centre * centre, axis=-1, keepdims=True)
    return centre * lax.rsqrt(spread + 1e-05) * gain + shift


def build_graph(neighbours, counts, coords, length):
    tokens_row = counts.shape[0]
    positions = jnp.arange(tokens_row, dtype=jnp.int32)
    later = positions >= length
    slots = jnp.arange(neighbours.shape[0], dtype=jnp.int32)[:, None]
    valid = (slots < counts[None, :]) & ((neighbours >= length) == later[None, :])

    def add_slot(slot, total):
        hit = (neighbours[slot][:, None] == positions[None, :]) & valid[slot][:, None]
        return total + hit.astype(jnp.float32)

    adjacency = lax.fori_loop(
        0, neighbours.shape[0], add_slot, jnp.zeros((tokens_row, tokens_row), jnp.float32)
    )
    inverse = 1.0 / counts.astype(jnp.float32)
    points = coords.T
    edge = (
        jnp.dot(adjacency, points, precision=lax.Precision.HIGHEST)
        - jnp.sum(adjacency, axis=1)[:, None] * points
    ) * inverse[:, None]
    delta_x = coords[0][None, :] - coords[0][:, None]
    delta_y = coords[1][None, :] - coords[1][:, None]
    distance = jnp.log(1.0 + 16.0 * (delta_x * delta_x + delta_y * delta_y))
    order = jnp.tanh(4.0 * delta_x)
    allowed = (jnp.abs(positions[:, None] - positions[None, :]) <= RADIUS) & (
        later[:, None] == later[None, :]
    )
    return (adjacency.astype(jnp.bfloat16), inverse, edge, distance, order, allowed)


def split_heads(qkv_low, heads):
    tokens_row = qkv_low.shape[0]
    return qkv_low.reshape(tokens_row, 3, heads, -1).transpose(2, 1, 0, 3)


def head_scores(queries, keys_all, rate_dist, rate_order, distance, order, allowed):
    raw = dot_right_t(queries, keys_all) * 0.125
    raw = raw - rate_dist * distance + rate_order * order
    return jnp.where(allowed, raw, -1000000000.0)


def attention_forward(qkv_low, distance, order, allowed, distance_rate, order_rate):
    tokens_row = qkv_low.shape[0]
    heads = distance_rate.shape[0]
    per_head = split_heads(qkv_low, heads)

    def one_head(item):
        parts, rate_dist, rate_order = item
        scores = head_scores(parts[0], parts[1], rate_dist, rate_order, distance, order, allowed)
        peak = jnp.max(scores, axis=-1, keepdims=True)
        log_total = peak + jnp.log(jnp.sum(jnp.exp(scores - peak), axis=-1, keepdims=True))
        probs_low = jnp.exp(scores - log_total).astype(jnp.bfloat16)
        return (dot_plain(probs_low, parts[2]), log_total)

    attended, log_total = lax.map(one_head, (per_head, distance_rate, order_rate))
    attended = attended.transpose(1, 0, 2).reshape(tokens_row, -1).astype(jnp.bfloat16)
    return (attended, log_total)


def attention_backward(
    qkv_low, log_total, grad_attended, distance, order, allowed, distance_rate, order_rate
):
    tokens_row = qkv_low.shape[0]
    heads = distance_rate.shape[0]
    per_head = split_heads(qkv_low, heads)
    grad_heads = grad_attended.reshape(tokens_row, heads, -1).transpose(1, 0, 2)

    def one_head(item):
        parts, grad_head, total, rate_dist, rate_order = item
        queries, keys_all, values = (parts[0], parts[1], parts[2])
        scores = head_scores(queries, keys_all, rate_dist, rate_order, distance, order, allowed)
        probs = jnp.exp(scores - total)
        probs_low = probs.astype(jnp.bfloat16)
        grad_probs = dot_right_t(grad_head, values)
        grad_values = dot_left_t(probs_low, grad_head)
        grad_scores = probs * (grad_probs - jnp.sum(probs * grad_probs, axis=-1, keepdims=True))
        scores_low = grad_scores.astype(jnp.bfloat16)
        scores_wide = scores_low.astype(jnp.float32)
        grad_rate = -jnp.sum(scores_wide * distance)
        grad_order = jnp.sum(scores_wide * order)
        grad_queries = dot_plain(scores_low, keys_all) * 0.125
        grad_keys = dot_left_t(scores_low, queries) * 0.125
        return (jnp.stack([grad_queries, grad_keys, grad_values]), grad_rate, grad_order)

    stacked, grad_rate, grad_order = lax.map(
        one_head, (per_head, grad_heads, log_total, distance_rate, order_rate)
    )
    stacked = stacked.transpose(2, 1, 0, 3).reshape(tokens_row, -1).astype(jnp.bfloat16)
    return (stacked, grad_rate, grad_order)


def forward_layer(
    inputs,
    graph,
    graph_full,
    block_full,
    edge_proj,
    norm_gains,
    norm_shifts,
    distance_rate,
    order_rate,
):
    adj_low, inverse, edge, distance, order, allowed = graph
    self_one, near_one, self_two, near_two = graph_full
    qkv_proj, out_proj, up_proj, down_proj = block_full
    agg_one = (inverse[:, None] * dot_plain(adj_low, inputs)).astype(jnp.bfloat16)
    pre_one = dot_plain(inputs, self_one) + dot_plain(agg_one, near_one)
    pre_one = pre_one + jnp.dot(edge, edge_proj, precision=lax.Precision.HIGHEST)
    hidden_one = jax.nn.gelu(pre_one).astype(jnp.bfloat16)
    agg_two = (inverse[:, None] * dot_plain(adj_low, hidden_one)).astype(jnp.bfloat16)
    resid_one = (
        inputs.astype(jnp.float32) + dot_plain(hidden_one, self_two) + dot_plain(agg_two, near_two)
    )
    normed_one = layer_norm(resid_one, norm_gains[0], norm_shifts[0])
    normed_low = normed_one.astype(jnp.bfloat16)
    qkv_low = dot_plain(normed_low, qkv_proj).astype(jnp.bfloat16)
    attended, log_total = attention_forward(
        qkv_low, distance, order, allowed, distance_rate, order_rate
    )
    resid_two = normed_one + dot_plain(attended, out_proj)
    normed_two = layer_norm(resid_two, norm_gains[1], norm_shifts[1])
    second_low = normed_two.astype(jnp.bfloat16)
    up_pre = dot_plain(second_low, up_proj)
    activated = jax.nn.gelu(up_pre).astype(jnp.bfloat16)
    resid_three = normed_two + dot_plain(activated, down_proj)
    result = layer_norm(resid_three, norm_gains[2], norm_shifts[2]).astype(jnp.bfloat16)
    kept = (
        agg_one,
        pre_one,
        hidden_one,
        agg_two,
        resid_one,
        normed_low,
        qkv_low,
        log_total,
        attended,
        resid_two,
        second_low,
        up_pre,
        activated,
        resid_three,
    )
    return (result, kept)


def backward_layer(
    inputs,
    graph,
    kept,
    grad_output,
    graph_full,
    block_full,
    norm_gains,
    norm_shifts,
    distance_rate,
    order_rate,
):
    adj_low, inverse, edge, distance, order, allowed = graph
    self_one, near_one, self_two, near_two = graph_full
    qkv_proj, out_proj, up_proj, down_proj = block_full
    (
        agg_one,
        pre_one,
        hidden_one,
        agg_two,
        resid_one,
        normed_low,
        qkv_low,
        log_total,
        attended,
        resid_two,
        second_low,
        up_pre,
        activated,
        resid_three,
    ) = kept
    norm_back = jax.vjp(layer_norm, resid_three, norm_gains[2], norm_shifts[2])[1]
    grad_three, gain_three, shift_three = norm_back(grad_output)
    down_low = grad_three.astype(jnp.bfloat16)
    grad_down = dot_left_t(activated, down_low)
    gelu_back = jax.vjp(jax.nn.gelu, up_pre)[1]
    up_low = gelu_back(dot_right_t(down_low, down_proj))[0].astype(jnp.bfloat16)
    grad_up = dot_left_t(second_low, up_low)
    grad_normed_two = grad_three + dot_right_t(up_low, up_proj)
    norm_back = jax.vjp(layer_norm, resid_two, norm_gains[1], norm_shifts[1])[1]
    grad_two, gain_two, shift_two = norm_back(grad_normed_two)
    attn_low = grad_two.astype(jnp.bfloat16)
    grad_out = dot_left_t(attended, attn_low)
    grad_attended = dot_right_t(attn_low, out_proj).astype(jnp.bfloat16)
    qkv_grad_low, grad_rate, grad_order = attention_backward(
        qkv_low, log_total, grad_attended, distance, order, allowed, distance_rate, order_rate
    )
    grad_qkv = dot_left_t(normed_low, qkv_grad_low)
    grad_normed_one = grad_two + dot_right_t(qkv_grad_low, qkv_proj)
    norm_back = jax.vjp(layer_norm, resid_one, norm_gains[0], norm_shifts[0])[1]
    grad_one, gain_one, shift_one = norm_back(grad_normed_one)
    branch_low = grad_one.astype(jnp.bfloat16)
    grad_self_two = dot_left_t(hidden_one, branch_low)
    grad_near_two = dot_left_t(agg_two, branch_low)
    mean_low = (inverse[:, None] * dot_right_t(branch_low, near_two)).astype(jnp.bfloat16)
    grad_hidden = dot_right_t(branch_low, self_two) + dot_left_t(adj_low, mean_low)
    gelu_back = jax.vjp(jax.nn.gelu, pre_one)[1]
    grad_pre = gelu_back(grad_hidden)[0]
    grad_edge = jnp.dot(edge.T, grad_pre, precision=lax.Precision.HIGHEST)
    pre_low = grad_pre.astype(jnp.bfloat16)
    grad_self_one = dot_left_t(inputs, pre_low)
    grad_near_one = dot_left_t(agg_one, pre_low)
    first_low = (inverse[:, None] * dot_right_t(pre_low, near_one)).astype(jnp.bfloat16)
    grad_inputs = grad_one + dot_right_t(pre_low, self_one) + dot_left_t(adj_low, first_low)
    gains_back = jnp.stack([gain_one, gain_two, gain_three])
    shifts_back = jnp.stack([shift_one, shift_two, shift_three])
    return (
        grad_inputs,
        (grad_self_one, grad_near_one, grad_self_two, grad_near_two),
        (grad_qkv, grad_out, grad_up, grad_down),
        (grad_edge, gains_back, shifts_back, grad_rate, grad_order),
    )


def add_trees(first, second):
    if first is None:
        return second
    return jax.tree.map(lambda left, right: left + right, first, second)


def local(
    inputs,
    coords,
    neighbours,
    counts,
    doc_length,
    self_one,
    near_one,
    self_two,
    near_two,
    edge_proj,
    qkv_proj,
    out_proj,
    up_proj,
    down_proj,
    norm_gains,
    norm_shifts,
    distance_rate,
    order_rate,
    cotangent,
):

    def fetch_graph():
        return (
            lax.all_gather(self_one, ("wide", "narrow"), axis=0, tiled=True),
            lax.all_gather(near_one, ("wide", "narrow"), axis=0, tiled=True),
            lax.all_gather(self_two, ("wide", "narrow"), axis=0, tiled=True),
            lax.all_gather(near_two, ("wide", "narrow"), axis=0, tiled=True),
        )

    def fetch_block():
        return (
            lax.all_gather(qkv_proj, ("wide", "narrow"), axis=0, tiled=True),
            lax.all_gather(out_proj, ("wide", "narrow"), axis=0, tiled=True),
            lax.all_gather(up_proj, ("wide", "narrow"), axis=0, tiled=True),
            lax.all_gather(down_proj, ("wide", "narrow"), axis=0, tiled=True),
        )

    results = []
    input_grads = []
    graph_total = None
    block_total = None
    small_total = None
    for member in range(inputs.shape[0]):
        graph = build_graph(
            neighbours[member], counts[member], coords[member], doc_length[member, 0]
        )
        result, kept = forward_layer(
            inputs[member],
            graph,
            fetch_graph(),
            fetch_block(),
            edge_proj,
            norm_gains,
            norm_shifts,
            distance_rate,
            order_rate,
        )
        results.append(result)
        grad_inputs, graph_grads, block_grads, small_grads = backward_layer(
            inputs[member],
            graph,
            kept,
            cotangent[member].astype(jnp.float32),
            fetch_graph(),
            fetch_block(),
            norm_gains,
            norm_shifts,
            distance_rate,
            order_rate,
        )
        input_grads.append(grad_inputs)
        small_total = add_trees(small_total, small_grads)
        graph_total = add_trees(graph_total, graph_grads)
        block_total = add_trees(block_total, block_grads)
    graph_total = lax.psum_scatter(graph_total, ("wide", "narrow"), scatter_dimension=0, tiled=True)
    block_total = lax.psum_scatter(block_total, ("wide", "narrow"), scatter_dimension=0, tiled=True)
    edge_sum, gains_sum, shifts_sum, rate_sum, order_sum = lax.psum(small_total, ("wide", "narrow"))
    return (
        jnp.stack(results),
        jnp.stack(input_grads),
        graph_total[0],
        graph_total[1],
        graph_total[2],
        graph_total[3],
        edge_sum,
        block_total[0],
        block_total[1],
        block_total[2],
        block_total[3],
        gains_sum,
        shifts_sum,
        rate_sum,
        order_sum,
    )


def solution(mesh):
    placed = (
        P(None, ("wide", "narrow"), None),
        P(None, None, ("wide", "narrow")),
        P(None, None, ("wide", "narrow")),
        P(None, ("wide", "narrow")),
        P(None, ("wide", "narrow")),
        P(("wide", "narrow"), None),
        P(("wide", "narrow"), None),
        P(("wide", "narrow"), None),
        P(("wide", "narrow"), None),
        P(),
        P(("wide", "narrow"), None),
        P(("wide", "narrow"), None),
        P(("wide", "narrow"), None),
        P(("wide", "narrow"), None),
        P(),
        P(),
        P(),
        P(),
        P(None, ("wide", "narrow"), None),
    )
    return jax.shard_map(
        local,
        mesh=mesh,
        in_specs=placed,
        out_specs=(
            P(None, ("wide", "narrow"), None),
            P(None, ("wide", "narrow"), None),
            P(("wide", "narrow"), None),
            P(("wide", "narrow"), None),
            P(("wide", "narrow"), None),
            P(("wide", "narrow"), None),
            P(),
            P(("wide", "narrow"), None),
            P(("wide", "narrow"), None),
            P(("wide", "narrow"), None),
            P(("wide", "narrow"), None),
            P(),
            P(),
            P(),
            P(),
        ),
        check_vma=False,
    )
```

profile of v0, /device:TPU:0, one launch (start us, length us, event | category | flops | bytes accessed | tf_op | source)
XLA Modules:
  0.0 2082.8 jit_solution(10285148780879893163)
XLA Ops:
  21.9 147.4 %while.88 = (s32[]{:T(128)}, f32[768,768]{1,0:T(8,128)}, s32[40,768]{1,0:T(8,128)S(1)}, pred[40,768]{1,0:T(8,128)(4,1)S(1)}, s32[]{:T(128)}, /*index=5*/s32[]{:T(128)}) while((s32[]{:T(128)}, f32[768,768]{1,0:T(8,128)}, s32[40,768]{1,0:T(8,128)S(1)}, pred[40,768]{1,0:T(8,128)(4,1)S(1)}, s32[]{:T(128)}, /*index=5*/s32[]{:T(128)}) %tuple.238), condition=%wide.region_1.0_spmd.clone, body=%wide.region_0.0_spmd.clone.sunk | while | flops 2949123 | bytes 4730199 | solution.py:42
  187.6 93.1 %while.89 = (s32[]{:T(128)}, f32[768,768]{1,0:T(8,128)S(1)}, s32[40,768]{1,0:T(8,128)}, pred[40,768]{1,0:T(8,128)(4,1)}, s32[]{:T(128)}, /*index=5*/s32[]{:T(128)}) while((s32[]{:T(128)}, f32[768,768]{1,0:T(8,128)S(1)}, s32[40,768]{1,0:T(8,128)}, pred[40,768]{1,0:T(8,128)(4,1)}, s32[]{:T(128)}, /*index=5*/s32[]{:T(128)}) %tuple.232), condition=%wide.region_14.15_spmd.clone, body=%wide.region_13.14_spmd.clone.sunk | while | flops 2949123 | bytes 4730199 | solution.py:42
  324.3 6.8 convolution_convert_fusion.1
  331.0 5.8 copy.79
  336.8 8.0 copy.80
  346.6 127.4 %while.90 = (s32[]{:T(128)}, bf16[12,768,64]{1,2,0:T(8,128)(2,1)}, f32[12,768,1]{1,2,0:T(1,128)}, bf16[12,3,768,64]{3,2,1,0:T(8,128)(2,1)}, f32[12]{0:T(128)}, /...) while((s32[]{:T(128)}, bf16[12,768,64]{1,2,0:T(8,128)(2,1)}, ...), condition=%wide.region_8.9_spmd.clone.clone, body=%wide.region_5.8_spmd.clone.clone.sunk | while | flops 165149952 | bytes 7914165 | solution.py:85
  474.0 7.8 convolution_convert_fusion
  481.8 5.8 copy.82
  487.6 8.1 copy.83
  497.5 127.3 %while.91 = (s32[]{:T(128)}, bf16[12,768,64]{1,2,0:T(8,128)(2,1)}, f32[12,768,1]{1,2,0:T(1,128)}, bf16[12,3,768,64]{3,2,1,0:T(8,128)(2,1)}, f32[12]{0:T(128)}, /...) while((s32[]{:T(128)}, bf16[12,768,64]{1,2,0:T(8,128)(2,1)}, ...), condition=%wide.region_21.22_spmd.clone.clone, body=%wide.region_18.21_spmd.clone.clone.sunk | while | flops 165149952 | bytes 7914165 | solution.py:85
  635.6 8.9 fusion.220
  644.6 10.3 fusion.245
  654.9 7.1 fusion.214
  662.1 10.0 fusion.246
  679.3 13.7 fusion.136
  693.0 13.8 fusion.143
  706.9 6.6 add_add_fusion.11
  713.7 6.0 multiply_reduce_fusion.4
  735.3 247.7 %while.92 = (s32[]{:T(128)}, bf16[12,3,768,64]{2,3,0,1:T(8,128)(2,1)}, f32[12]{0:T(128)S(1)}, f32[12]{0:T(128)}, bf16[12,3,768,64]{3,2,1,0:T(8,128)(2,1)}, /*ind...) while((s32[]{:T(128)}, ...), condition=%wide.region_34.35_spmd.clone.clone, body=%wide.region_30.34_spmd.clone.clone.sunk | while | flops 401571072 | bytes 20002484 | solution.py:115
  740.1 5.5 multiply_reduce_fusion.18
  760.8 5.5 multiply_reduce_fusion.18
  802.1 5.5 multiply_reduce_fusion.18
  822.7 5.5 multiply_reduce_fusion.18
  843.3 5.5 multiply_reduce_fusion.18
  905.2 5.5 multiply_reduce_fusion.18
  946.4 5.5 multiply_reduce_fusion.18
  967.1 5.5 multiply_reduce_fusion.18
  990.6 241.5 %while.93 = (s32[]{:T(128)}, bf16[12,3,768,64]{2,3,0,1:T(8,128)(2,1)}, f32[12]{0:T(128)S(1)}, f32[12]{0:T(128)S(1)}, bf16[12,3,768,64]{3,2,1,0:T(8,128)(2,1)}, /...) while((s32[]{:T(128)}, ...), condition=%wide.region_45.46_spmd.clone.clone, body=%wide.region_41.45_spmd.clone.clone.sunk | while | flops 401571072 | bytes 20002044 | solution.py:115
  1055.5 5.5 multiply_reduce_fusion.19
  1075.6 5.5 multiply_reduce_fusion.19
  1196.1 5.5 multiply_reduce_fusion.19
  1232.7 6.8 add_add_fusion.10
  1265.1 9.5 fusion.248
  1281.5 9.6 fusion.247
  1317.9 10.3 fusion.191
  1328.3 11.6 convolution_add_fusion.1
  1341.6 6.3 fusion.218
  1347.9 9.0 convolution_add_fusion.2
  1370.0 8.5 add_bitcast_fusion.2
  1378.5 8.1 add_bitcast_fusion.1
  1391.5 6.2 copy.101
  1406.5 43.0 %all-reduce = (f32[2,768]{1,0:T(2,128)}, f32[3,768]{1,0:T(4,128)}, f32[3,768]{1,0:T(4,128)}, f32[12]{0:T(128)}, f32[12]{0:T(128)}) all-reduce(f32[2,768]{1,0:T(2,128)S(1)} %convolution_add_fusion.7, f32[3,768]{1,0:T(4,128)S(1)} %maximum_add_fusion, ...), channel_id=1, replica_groups=mesh['wide'=16,'narrow'=2] {'wide','narrow'}, use_global_device_ids=true, to_apply=%region_52.53 | all-reduce | flops 6168 | bytes 49344 | tf_op jit(solution)/shard_map/psum | solution.py:333
  1449.5 9.6 reduce-scatter.13.cloned.1.call-done
  1459.1 104.6 %reduce-scatter.11.cloned.1.call-done = f32[24,768]{1,0:T(8,128)} async-done(((f32[768,768]{1,0:T(8,128)}), f32[24,768]{1,0:T(8,128)}) %reduce-scatter.11.cloned.1.call-update) | async-done | bytes 73744 | tf_op jit(solution)/shard_map/reduce_scatter | solution.py:331
  1563.8 103.9 %reduce-scatter.25.cloned.1.call-done = f32[24,768]{1,0:T(8,128)} async-done(((f32[768,768]{1,0:T(8,128)}), f32[24,768]{1,0:T(8,128)}) %reduce-scatter.25.cloned.1.call-update) | async-done | bytes 73744
  1667.7 125.2 %reduce-scatter.17.cloned.1.call-done = f32[24,2304]{1,0:T(8,128)} async-done(((f32[768,2304]{1,0:T(8,128)}), f32[24,2304]{1,0:T(8,128)}) %reduce-scatter.17.cloned.1.call-update) | async-done | bytes 221200 | tf_op jit(solution)/shard_map/reduce_scatter | solution.py:332
  1792.9 141.3 %reduce-scatter.23.cloned.1.call-done = f32[96,768]{1,0:T(8,128)} async-done(((f32[3072,768]{1,0:T(8,128)}), f32[96,768]{1,0:T(8,128)}) %reduce-scatter.23.cloned.1.call-update) | async-done | bytes 294928 | tf_op jit(solution)/shard_map/reduce_scatter | solution.py:332
  1934.2 141.9 %reduce-scatter.21.cloned.1.call-done = f32[24,3072]{1,0:T(8,128)} async-done(((f32[768,3072]{1,0:T(8,128)}), f32[24,3072]{1,0:T(8,128)}) %reduce-scatter.21.cloned.1.call-update) | async-done | bytes 294928 | tf_op jit(solution)/shard_map/reduce_scatter | solution.py:332
  (1271 shorter events, 1113.2 us)
Async XLA Ops:
  7.2 288.8 %copy-start = (f32[2,768]{1,0:T(2,128)S(1)}, f32[2,768]{1,0:T(2,128)}, u32[]{:S(2)}) copy-start(f32[2,768]{1,0:T(2,128)} %param.40) | copy-start | bytes 18436
  7.2 282.0 %all-gather.9.cloned.1.call-start = ((), (), s32[]{:S(2)}) async-start(), calls=%async_computation.8 | async-start | bytes 1216512 | tf_op jit(solution)/shard_map/all_gather | solution.py:280
  7.9 285.6 %all-gather.11.cloned.1.call-start = ((), (), s32[]{:S(2)}) async-start(), calls=%async_computation.9 | async-start | bytes 1216512 | tf_op jit(solution)/shard_map/all_gather | solution.py:281
  8.7 292.0 %all-gather.13.cloned.1.call-start = ((), (), s32[]{:S(2)}) async-start(), calls=%async_computation.10 | async-start | bytes 1216512 | tf_op jit(solution)/shard_map/all_gather | solution.py:282
  9.4 295.4 %all-gather.15.cloned.1.call-start = ((), (), s32[]{:S(2)}) async-start(), calls=%async_computation.11 | async-start | bytes 1216512 | tf_op jit(solution)/shard_map/all_gather | solution.py:283
  10.0 314.3 %all-gather.17.cloned.1.call-start = ((), (), s32[]{:S(2)}) async-start(), calls=%async_computation.12 | async-start | bytes 3649536 | tf_op jit(solution)/shard_map/all_gather | solution.py:288
  10.6 614.3 %all-gather.19.cloned.1.call-start = ((), (), s32[]{:S(2)}) async-start(), calls=%async_computation.13 | async-start | bytes 1216512 | tf_op jit(solution)/shard_map/all_gather | solution.py:289
  11.2 624.5 %all-gather.21.cloned.1.call-start = ((), (), s32[]{:S(2)}) async-start(), calls=%async_computation.14 | async-start | bytes 4866048 | tf_op jit(solution)/shard_map/all_gather | solution.py:290
  11.9 632.7 %all-gather.23.cloned.1.call-start = ((), (), s32[]{:S(2)}) async-start(), calls=%async_computation.15 | async-start | bytes 4866048 | tf_op jit(solution)/shard_map/all_gather | solution.py:291
  12.7 1436.9 %reduce-scatter.19.cloned.1.call-start = ((), (), s32[]{:S(2)}) async-start(), calls=%async_computation.20 | async-start | bytes 2433024 | tf_op jit(solution)/shard_map/reduce_scatter | solution.py:332
  18.9 158.7 %copy-start.110 = (f32[768]{0:T(1024)}, f32[768]{0:T(1024)S(1)}, u32[]{:S(2)}) copy-start(f32[768]{0:T(1024)S(1)} %get-tuple-element.1044) | copy-start | bytes 9220
  288.5 418.4 %copy-start.16 = (bf16[1,768,768]{1,2,0:T(8,128)(2,1)}, bf16[1,768,768]{1,2,0:T(8,128)(2,1)S(1)}, u32[]{:S(2)}) copy-start(bf16[1,768,768]{1,2,0:T(8,128)(2,1)S(1)} %copy.120) | copy-start | bytes 3538948
  289.2 372.8 %copy-start.62 = (f32[768]{0:T(1024)}, f32[768]{0:T(1024)S(1)}, u32[]{:S(2)}) copy-start(f32[768]{0:T(1024)S(1)} %get-tuple-element.867) | copy-start | bytes 9220
  289.2 430.5 %copy-start.60 = (f32[768]{0:T(1024)}, f32[768]{0:T(1024)S(1)}, u32[]{:S(2)}) copy-start(f32[768]{0:T(1024)S(1)} %get-tuple-element.1047) | copy-start | bytes 9220
  308.9 15.4 copy-start.3
  628.8 91.0 %copy-start.9 = (f32[768,768]{0,1:T(8,128)}, f32[768,768]{0,1:T(8,128)S(1)}, u32[]{:S(2)}) copy-start(f32[768,768]{0,1:T(8,128)S(1)} %get-tuple-element.1032) | copy-start | bytes 7077892
  628.9 90.9 %copy-start.68 = (f32[768]{0:T(1024)}, f32[768]{0:T(1024)S(1)}, u32[]{:S(2)}) copy-start(f32[768]{0:T(1024)S(1)} %broadcast_multiply_fusion.4) | copy-start | bytes 9220
  632.7 87.0 %copy-start.70 = (f32[768]{0:T(1024)}, f32[768]{0:T(1024)S(1)}, u32[]{:S(2)}) copy-start(f32[768]{0:T(1024)S(1)} %broadcast_multiply_fusion.1) | copy-start | bytes 9220
  644.6 10.3 copy-start.12
  644.6 10.3 copy-start.19
  644.6 10.3 copy-start.72
  654.8 58.7 %copy-start.20 = (f32[768,768]{0,1:T(8,128)}, f32[768,768]{0,1:T(8,128)S(1)}, u32[]{:S(2)}) copy-start(f32[768,768]{0,1:T(8,128)S(1)} %get-tuple-element.1034) | copy-start | bytes 7077892
  654.9 58.7 %copy-start.84 = (f32[768]{0:T(1024)}, f32[768]{0:T(1024)S(1)}, u32[]{:S(2)}) copy-start(f32[768]{0:T(1024)S(1)} %broadcast_multiply_fusion.3) | copy-start | bytes 9220
  672.1 34.8 %copy-start.21 = (f32[768,768]{0,1:T(8,128)}, f32[768,768]{0,1:T(8,128)S(1)}, u32[]{:S(2)}) copy-start(f32[768,768]{0,1:T(8,128)S(1)} %get-tuple-element.1036) | copy-start | bytes 7077892
  672.1 34.7 %copy-start.94 = (f32[768]{0:T(1024)}, f32[768]{0:T(1024)S(1)}, u32[]{:S(2)}) copy-start(f32[768]{0:T(1024)S(1)} %broadcast_multiply_fusion) | copy-start | bytes 9220
  672.8 40.8 %copy-start.114 = (f32[768]{0:T(1024)}, f32[768]{0:T(1024)S(1)}, u32[]{:S(2)}) copy-start(f32[768]{0:T(1024)S(1)} %get-tuple-element.1021) | copy-start | bytes 9220
  672.8 40.8 %copy-start.116 = (f32[768]{0:T(1024)}, f32[768]{0:T(1024)S(1)}, u32[]{:S(2)}) copy-start(f32[768]{0:T(1024)S(1)} %get-tuple-element.1022) | copy-start | bytes 9220
  676.3 37.3 %copy-start.157 = (f32[768]{0:T(1024)}, f32[768]{0:T(1024)S(1)}, u32[]{:S(2)}) copy-start(f32[768]{0:T(1024)S(1)} %negate_multiply_fusion.5) | copy-start | bytes 9220
  676.4 30.5 %copy-start.123 = (f32[768]{0:T(1024)}, f32[768]{0:T(1024)S(1)}, u32[]{:S(2)}) copy-start(f32[768]{0:T(1024)S(1)} %get-tuple-element.1019) | copy-start | bytes 9220
  676.4 30.5 %copy-start.125 = (f32[768]{0:T(1024)}, f32[768]{0:T(1024)S(1)}, u32[]{:S(2)}) copy-start(f32[768]{0:T(1024)S(1)} %get-tuple-element.1020) | copy-start | bytes 9220
  679.3 27.6 %copy-start.159 = (f32[768]{0:T(1024)}, f32[768]{0:T(1024)S(1)}, u32[]{:S(2)}) copy-start(f32[768]{0:T(1024)S(1)} %negate_multiply_fusion.2) | copy-start | bytes 9220
  721.1 261.9 %copy-start.103 = (f32[768]{0:T(1024)}, f32[768]{0:T(1024)S(1)}, u32[]{:S(2)}) copy-start(f32[768]{0:T(1024)S(1)} %negate_multiply_fusion.1) | copy-start | bytes 9220
  725.9 723.7 %reduce-scatter.15.cloned.1.call-start = ((), (), s32[]{:S(2)}) async-start(), calls=%async_computation.18 | async-start | bytes 2433024 | tf_op jit(solution)/shard_map/reduce_scatter | solution.py:331
  735.3 247.7 %copy-start.172 = (bf16[768,768]{1,0:T(8,128)(2,1)S(1)}, bf16[768,768]{1,0:T(8,128)(2,1)}, u32[]{:S(2)}) copy-start(bf16[768,768]{1,0:T(8,128)(2,1)} %all-gather.19.cloned.1.call-done) | copy-start | bytes 3538948
  990.6 242.1 %copy-start.104 = (f32[768]{0:T(1024)S(1)}, f32[768]{0:T(1024)}, u32[]{:S(2)}) copy-start(f32[768]{0:T(1024)} %copy-done.103) | copy-start | bytes 9220
  1253.4 205.7 %reduce-scatter.13.cloned.1.call-start = ((), (), s32[]{:S(2)}) async-start(), calls=%async_computation.17 | async-start | bytes 2433024 | tf_op jit(solution)/shard_map/reduce_scatter | solution.py:331
  1260.6 303.2 %reduce-scatter.11.cloned.1.call-start = ((), (), s32[]{:S(2)}) async-start(), calls=%async_computation.16 | async-start | bytes 2433024 | tf_op jit(solution)/shard_map/reduce_scatter | solution.py:331
  1296.5 371.2 %reduce-scatter.25.cloned.1.call-start = ((), (), s32[]{:S(2)}) async-start(), calls=%async_computation.23 | async-start | bytes 2433024
  1305.2 487.7 %reduce-scatter.17.cloned.1.call-start = ((), (), s32[]{:S(2)}) async-start(), calls=%async_computation.19 | async-start | bytes 7299072 | tf_op jit(solution)/shard_map/reduce_scatter | solution.py:332
  1316.6 11.6 copy-start.17
  1316.6 11.6 copy-start.95
  1316.6 11.6 copy-start.124
  1316.6 11.6 copy-start.126
  1316.7 11.6 copy-start.160
  1316.7 617.5 %reduce-scatter.23.cloned.1.call-start = ((), (), s32[]{:S(2)}) async-start(), calls=%async_computation.22 | async-start | bytes 9732096 | tf_op jit(solution)/shard_map/reduce_scatter | solution.py:332
  1317.9 10.4 copy-start.22
  1339.9 736.2 %reduce-scatter.21.cloned.1.call-start = ((), (), s32[]{:S(2)}) async-start(), calls=%async_computation.21 | async-start | bytes 9732096 | tf_op jit(solution)/shard_map/reduce_scatter | solution.py:332
  1402.2 673.8 %copy-start.1 = (f32[2,768]{1,0:T(2,128)S(1)}, f32[2,768]{1,0:T(2,128)}, u32[]{:S(2)}) copy-start(f32[2,768]{1,0:T(2,128)} %param.40) | copy-start | bytes 18436
  (178 other events, 619.1 us)
Sparse Core Ops, SparseCore 0:
  10.9 56.8 all-gather.8
  70.7 53.0 all-gather.10
  126.8 53.0 all-gather.12
  182.7 53.0 all-gather.14
  238.5 59.0 all-gather.16
  300.5 52.9 all-gather.18
  356.4 62.5 all-gather.20
  421.9 62.4 all-gather.22
  726.0 101.4 reduce-scatter.18
  1253.5 101.5 reduce-scatter.14
  1361.0 98.1 reduce-scatter.12
  1465.7 98.0 reduce-scatter.10
  1569.6 98.0 reduce-scatter.24
  1674.7 118.1 reduce-scatter.16
  1799.2 134.9 reduce-scatter.22
  1941.5 134.4 reduce-scatter.20
where the time goes:
time: 2100 us; the launch traced here: 2080 us
  matrix products  720 us (34%)
  waiting for transfers between devices  632 us (30%)
  local copies, waits for them, and re-layouts  335 us (16%)
  other arithmetic  317 us (15%)
  blocking collectives  43 us (2%)
    reduce_scatter x4, waiting for transfers between devices, local(): lax.psum_scatter(block_total, ('wide', 'narrow'), scatter_dimension=0, ti...  408 us
    dot_general x84, matrix products, dot_right_t(): lax.dot_general(left, right, (((1,), (1,)), ((), ())), preferred_element_...  358 us
    dot_general x68, matrix products, dot_left_t(): lax.dot_general(left, right, (((0,), (0,)), ((), ())), preferred_element_...  183 us
    add x80, other arithmetic, add_slot(): return total + hit.astype(jnp.float32)  178 us
    dot_general x68, matrix products, dot_plain(): return jnp.dot(left, right, preferred_element_type=jnp.float32)  165 us
    dynamic_slice x96, local copies, waits for them, and re-layouts, attention_forward(): lax.map(one_head, (per_head, distance_rate, order_rate))  119 us
    reduce_scatter x3, waiting for transfers between devices, local(): lax.psum_scatter(graph_total, ('wide', 'narrow'), scatter_dimension=0, ti...  114 us
    unnamed x17, waiting for transfers between devices  109 us
  transfers between devices with their start and end apart: 16, of which 6 were waited for; matrix products, arithmetic and copies ran while one was open for 61% of the time, Pallas kernels for 0%

commit v1 on v0

v1 whole, which is shorter than its diff:
```python
import functools
import jax
import jax.numpy as jnp
from jax import lax
from jax.experimental import pallas as pl
from jax.experimental.pallas import tpu as pltpu
from jax.sharding import PartitionSpec as P

RADIUS = 128
REACH = 64
BLOCK = 128
WIDE = BLOCK + 2 * REACH
SPAN = BLOCK + 2 * RADIUS
FAR = 1e10
F32 = jnp.float32
LOW = jnp.bfloat16
VMEM = 60 * 2**20


def dot(left, right, dims):
    return lax.dot_general(left, right, ((dims[:1], dims[1:]), ((), ())), preferred_element_type=F32)


def nn(left, right):
    return dot(left, right, (1, 0))


def nt(left, right):
    return dot(left, right, (1, 1))


def tn(left, right):
    return dot(left, right, (0, 0))


def gelu_pair(pre):
    slope = 0.7978845608028654
    square = pre * pre
    half = 0.5 + 0.5 * jnp.tanh(pre * (slope + (slope * 0.044715) * square))
    act = pre * half
    deriv = half + act * (1.0 - half) * (2.0 * slope + (6.0 * slope * 0.044715) * square)
    return act, deriv


def norm_parts(values):
    centre = values - jnp.mean(values, axis=-1, keepdims=True)
    rstd = lax.rsqrt(jnp.mean(centre * centre, axis=-1, keepdims=True) + 1e-05)
    return centre * rstd, rstd


def norm_back(grad, unit, rstd, gain):
    scaled = grad * gain
    mean = jnp.mean(scaled, axis=-1, keepdims=True)
    along = jnp.mean(scaled * unit, axis=-1, keepdims=True)
    return rstd * (scaled - mean - unit * along)


def fold(values):
    rows, cols = values.shape
    return jnp.sum(values.reshape(rows // 8, 8, cols), axis=0)


def whole(shape, space=None):
    return pl.BlockSpec(shape, lambda *_: (0,) * len(shape), pipeline_mode=pl.Buffered(1))


def params(grid_rank, **more):
    return pltpu.CompilerParams(
        vmem_limit_bytes=VMEM, dimension_semantics=("arbitrary",) * grid_rank, **more
    )


def graph_kernel(
    length_ref, near_ref, count_ref, point_ref, x_ref, graph_ref, edge_w_ref, gain_ref, shift_ref,
    qkv_w_ref,
    adj_ref, cols_ref, agg1_ref, slope_ref, hidden_ref, agg2_ref, unit_ref, rstd_ref, normed_ref,
    low_ref, qkv_ref,
    pad_ref, point_pad, rel_ref,
):
    row = pl.program_id(0)
    slots, tokens = near_ref.shape[1:]
    width = x_ref.shape[2]
    blocks = tokens // BLOCK
    length = length_ref[row]
    zeros = jnp.zeros((REACH, width), LOW)
    pad_ref[pl.ds(0, REACH), :] = zeros
    pad_ref[pl.ds(tokens + REACH, REACH), :] = zeros
    pad_ref[pl.ds(REACH, tokens), :] = x_ref[0]
    points = point_ref[0]
    high = points.astype(LOW)
    rest = points - high.astype(F32)
    mid = rest.astype(LOW)
    tail = (rest - mid.astype(F32)).astype(LOW)
    split = jnp.concatenate(
        [high.astype(F32), mid.astype(F32), tail.astype(F32), jnp.ones((1, tokens), F32), jnp.zeros((9, tokens), F32)], axis=0
    )
    side = jnp.zeros((16, REACH), F32)
    point_pad[...] = jnp.concatenate([side, split, side], axis=1).astype(LOW)

    for b in range(blocks):
        lanes = slice(b * BLOCK, (b + 1) * BLOCK)
        near = near_ref[0, :, lanes]
        count = count_ref[0, :, lanes]
        place = lax.broadcasted_iota(jnp.int32, (1, BLOCK), 1) + b * BLOCK
        slot = lax.broadcasted_iota(jnp.int32, (slots, BLOCK), 0)
        same = (near >= length) == (place >= length)
        rel_ref[...] = jnp.where((slot < count) & same, near - (b * BLOCK - REACH), -1)
        spot = lax.broadcasted_iota(jnp.int32, (WIDE, BLOCK), 0)
        total = jnp.zeros((WIDE, BLOCK), F32)
        for s in range(slots):
            total = total + jnp.where(rel_ref[s : s + 1, :] == spot, 1.0, 0.0)
        adj = total.astype(LOW)
        adj_ref[0, b] = adj
        sums = nn(point_pad[:, b * BLOCK : b * BLOCK + WIDE], adj)
        inverse = 1.0 / count.astype(F32)
        here = points[:, lanes]
        edge = (sums[0:2] + sums[2:4] + sums[4:6] - sums[6:7] * here) * inverse
        lines = jnp.concatenate([edge, inverse, jnp.zeros((5, BLOCK), F32)], axis=0)
        cols = lines.T
        cols_ref[0, lanes, :] = cols
        agg = tn(adj, pad_ref[b * BLOCK : b * BLOCK + WIDE, :])
        agg1_ref[0, lanes, :] = (agg * cols[:, 2:3]).astype(LOW)

    chunk = 2 * BLOCK
    for c in range(tokens // chunk):
        part = slice(c * chunk, (c + 1) * chunk)
        pre = nn(x_ref[0, part, :], graph_ref[:, 0:width])
        pre = pre + nn(agg1_ref[0, part, :], graph_ref[:, width : 2 * width])
        pre = pre + cols_ref[0, part, 0:1] * edge_w_ref[0:1, :] + cols_ref[0, part, 1:2] * edge_w_ref[1:2, :]
        act, deriv = gelu_pair(pre)
        slope_ref[0, part, :] = deriv.astype(LOW)
        hidden_ref[0, part, :] = act.astype(LOW)
        pad_ref[REACH + c * chunk : REACH + (c + 1) * chunk, :] = act.astype(LOW)

    for b in range(blocks):
        lanes = slice(b * BLOCK, (b + 1) * BLOCK)
        agg = tn(adj_ref[0, b], pad_ref[b * BLOCK : b * BLOCK + WIDE, :])
        agg2_ref[0, lanes, :] = (agg * cols_ref[0, lanes, 2:3]).astype(LOW)

    for c in range(tokens // chunk):
        part = slice(c * chunk, (c + 1) * chunk)
        resid = x_ref[0, part, :].astype(F32) + nn(hidden_ref[0, part, :], graph_ref[:, 2 * width : 3 * width])
        resid = resid + nn(agg2_ref[0, part, :], graph_ref[:, 3 * width : 4 * width])
        unit, rstd = norm_parts(resid)
        unit_ref[0, part, :] = unit.astype(LOW)
        rstd_ref[0, part, :] = rstd
        normed = unit * gain_ref[0:1, :] + shift_ref[0:1, :]
        normed_ref[0, part, :] = normed
        low = normed.astype(LOW)
        low_ref[0, part, :] = low
        qkv_ref[0, part, :] = nn(low, qkv_w_ref[...]).astype(LOW)


def graph_forward(length, near, count, point, x, graph_w, edge_w, gains, shifts, qkv_w):
    rows, tokens, width = x.shape
    slots = near.shape[1]
    blocks = tokens // BLOCK
    wide = 3 * width
    per_row = lambda *shape: pl.BlockSpec((1,) + shape, lambda r: (r,) + (0,) * len(shape))
    out = lambda dtype, *shape: jax.ShapeDtypeStruct((rows,) + shape, dtype)
    return pl.pallas_call(
        graph_kernel,
        grid=(rows,),
        in_specs=[
            pl.BlockSpec(memory_space=pltpu.SMEM),
            per_row(slots, tokens),
            per_row(1, tokens),
            per_row(2, tokens),
            per_row(tokens, width),
            whole((width, 4 * width)),
            whole((2, width)),
            whole(gains.shape),
            whole(shifts.shape),
            whole((width, wide)),
        ],
        out_specs=[
            per_row(blocks, WIDE, BLOCK),
            per_row(tokens, 8),
            per_row(tokens, width),
            per_row(tokens, width),
            per_row(tokens, width),
            per_row(tokens, width),
            per_row(tokens, width),
            per_row(tokens, 1),
            per_row(tokens, width),
            per_row(tokens, width),
            per_row(tokens, wide),
        ],
        out_shape=[
            out(LOW, blocks, WIDE, BLOCK),
            out(F32, tokens, 8),
            out(LOW, tokens, width),
            out(LOW, tokens, width),
            out(LOW, tokens, width),
            out(LOW, tokens, width),
            out(LOW, tokens, width),
            out(F32, tokens, 1),
            out(F32, tokens, width),
            out(LOW, tokens, width),
            out(LOW, tokens, wide),
        ],
        scratch_shapes=[
            pltpu.VMEM((tokens + 2 * REACH, width), LOW),
            pltpu.VMEM((16, tokens + 2 * REACH), LOW),
            pltpu.VMEM((slots, BLOCK), jnp.int32),
        ],
        compiler_params=params(1),
        name="graph_forward",
    )(length, near, count, point, x, graph_w, edge_w, gains, shifts, qkv_w)


def fill_bias(length, point_ref, far_ref, order_ref):
    tokens = point_ref.shape[2]
    side = jnp.zeros((2, RADIUS), F32)
    padded = jnp.concatenate([side, point_ref[0], side], axis=1)
    tall = jnp.concatenate([padded, jnp.zeros((6, tokens + 2 * RADIUS), F32)], axis=0)
    for b in range(tokens // BLOCK):
        window = tall[:, b * BLOCK : b * BLOCK + SPAN].T
        key_x, key_y = window[:, 0:1], window[:, 1:2]
        lanes = slice(b * BLOCK, (b + 1) * BLOCK)
        delta_x = key_x - point_ref[0, 0:1, lanes]
        delta_y = key_y - point_ref[0, 1:2, lanes]
        dist = jnp.log(1.0 + 16.0 * (delta_x * delta_x + delta_y * delta_y))
        query = lax.broadcasted_iota(jnp.int32, (SPAN, BLOCK), 1) + b * BLOCK
        key = lax.broadcasted_iota(jnp.int32, (SPAN, BLOCK), 0) + (b * BLOCK - RADIUS)
        allowed = (jnp.abs(query - key) <= RADIUS) & ((query >= length) == (key >= length))
        allowed = allowed & (key >= 0) & (key < tokens)
        far_ref[b] = jnp.where(allowed, dist, FAR)
        order_ref[b] = jnp.tanh(4.0 * delta_x)


def pair_rows(values):
    lane = lax.broadcasted_iota(jnp.int32, values.shape, 1)
    zero = jnp.zeros_like(values)
    first = jnp.where(lane < BLOCK // 2, values, zero)
    second = jnp.where(lane < BLOCK // 2, zero, values)
    return jnp.concatenate([first, second], axis=0)


def pair_pick(values):
    lane = lax.broadcasted_iota(jnp.int32, (BLOCK, BLOCK), 1)
    return jnp.where(lane < BLOCK // 2, values[:BLOCK], values[BLOCK:])


def pad_rows(pad_ref, values):
    tokens = values.shape[0]
    zeros = jnp.zeros((RADIUS, values.shape[1]), pad_ref.dtype)
    pad_ref[pl.ds(0, RADIUS), :] = zeros
    pad_ref[pl.ds(RADIUS + tokens, RADIUS), :] = zeros
    pad_ref[pl.ds(RADIUS, tokens), :] = values


def attention_kernel(
    length_ref, dist_rate_ref, order_rate_ref, point_ref, q_ref, k_ref, v_ref,
    out_ref, probs_ref, far_out, order_out,
    keys, values,
):
    row, pair = pl.program_id(0), pl.program_id(1)

    @pl.when(pair == 0)
    def _():
        fill_bias(length_ref[row], point_ref, far_out.at[0], order_out.at[0])

    pad_rows(keys, k_ref[0])
    pad_rows(values, v_ref[0])
    for b in range(q_ref.shape[1] // BLOCK):
        lanes = slice(b * BLOCK, (b + 1) * BLOCK)
        window = slice(b * BLOCK, b * BLOCK + SPAN)
        queries = pair_rows(q_ref[0, lanes, :] * 0.125)
        raw = nt(keys[window, :], queries)
        far, order = far_out[0, b], order_out[0, b]
        sides = []
        for h in range(2):
            bias = order_rate_ref[2 * pair + h] * order - dist_rate_ref[2 * pair + h] * far
            scores = raw[:, h * BLOCK : (h + 1) * BLOCK] + bias
            grown = jnp.exp(scores - jnp.max(scores, axis=0, keepdims=True))
            scale = 1.0 / jnp.sum(grown, axis=0, keepdims=True)
            sides.append((grown * scale).astype(LOW))
        probs = jnp.concatenate(sides, axis=1)
        probs_ref[0, 0, b] = probs
        out_ref[0, lanes, :] = pair_pick(tn(probs, values[window, :])).astype(LOW)


def attention_forward(length, dist_rate, order_rate, point, qkv):
    rows, tokens, wide = qkv.shape
    width = wide // 3
    pairs = width // BLOCK
    blocks = tokens // BLOCK
    part = lambda k: pl.BlockSpec((1, tokens, BLOCK), lambda r, p: (r, 0, k * pairs + p))
    smem = pl.BlockSpec(memory_space=pltpu.SMEM)
    bias = pl.BlockSpec((1, blocks, SPAN, BLOCK), lambda r, p: (r, 0, 0, 0))
    return pl.pallas_call(
        attention_kernel,
        grid=(rows, pairs),
        in_specs=[smem, smem, smem, pl.BlockSpec((1, 2, tokens), lambda r, p: (r, 0, 0)), part(0), part(1), part(2)],
        out_specs=[
            part(0),
            pl.BlockSpec((1, 1, blocks, SPAN, 2 * BLOCK), lambda r, p: (r, p, 0, 0, 0)),
            bias,
            bias,
        ],
        out_shape=[
            jax.ShapeDtypeStruct((rows, tokens, width), LOW),
            jax.ShapeDtypeStruct((rows, pairs, blocks, SPAN, 2 * BLOCK), LOW),
            jax.ShapeDtypeStruct((rows, blocks, SPAN, BLOCK), F32),
            jax.ShapeDtypeStruct((rows, blocks, SPAN, BLOCK), F32),
        ],
        scratch_shapes=[pltpu.VMEM((tokens + 2 * RADIUS, BLOCK), LOW)] * 2,
        compiler_params=params(2),
        name="attention_forward",
    )(length, dist_rate, order_rate, point, qkv, qkv, qkv)


def attention_back_kernel(
    q_ref, k_ref, v_ref, grad_ref, probs_ref, far_ref, order_ref,
    dq_ref, dk_ref, dv_ref, rate_ref,
    keys, values, grad_keys, grad_values,
):
    pad_rows(keys, k_ref[0])
    pad_rows(values, v_ref[0])
    grad_keys[...] = jnp.zeros_like(grad_keys)
    grad_values[...] = jnp.zeros_like(grad_values)
    tokens = q_ref.shape[1]
    sums = [jnp.zeros((8, BLOCK), F32)] * 4
    for b in range(tokens // BLOCK):
        lanes = slice(b * BLOCK, (b + 1) * BLOCK)
        window = slice(b * BLOCK, b * BLOCK + SPAN)
        queries = pair_rows(q_ref[0, lanes, :] * 0.125)
        grads = pair_rows(grad_ref[0, lanes, :])
        probs_low = probs_ref[0, 0, b]
        back = nt(values[window, :], grads)
        dist = jnp.where(far_ref[0, b] < FAR, far_ref[0, b], 0.0)
        order = order_ref[0, b]
        sides = []
        for h in range(2):
            probs = probs_low[:, h * BLOCK : (h + 1) * BLOCK].astype(F32)
            part = back[:, h * BLOCK : (h + 1) * BLOCK]
            delta = jnp.sum(probs * part, axis=0, keepdims=True)
            scores = probs * (part - delta)
            sums[2 * h] = sums[2 * h] - fold(scores * dist)
            sums[2 * h + 1] = sums[2 * h + 1] + fold(scores * order)
            sides.append(scores.astype(LOW))
        scores_low = jnp.concatenate(sides, axis=1)
        grad_values[window, :] += nn(probs_low, grads)
        grad_keys[window, :] += nn(scores_low, queries)
        dq_ref[0, lanes, :] = (pair_pick(tn(scores_low, keys[window, :])) * 0.125).astype(LOW)
    dk_ref[0] = grad_keys[pl.ds(RADIUS, tokens), :].astype(LOW)
    dv_ref[0] = grad_values[pl.ds(RADIUS, tokens), :].astype(LOW)
    for k in range(4):
        rate_ref[0, 0, k] = sums[k]


def attention_backward(qkv, grad, probs, far, order):
    rows, tokens, wide = qkv.shape
    width = wide // 3
    pairs = width // BLOCK
    blocks = tokens // BLOCK
    part = lambda k: pl.BlockSpec((1, tokens, BLOCK), lambda r, p: (r, 0, k * pairs + p))
    bias = pl.BlockSpec((1, blocks, SPAN, BLOCK), lambda r, p: (r, 0, 0, 0))
    grads = jax.ShapeDtypeStruct((rows, tokens, width), LOW)
    return pl.pallas_call(
        attention_back_kernel,
        grid=(rows, pairs),
        in_specs=[
            part(0),
            part(1),
            part(2),
            part(0),
            pl.BlockSpec((1, 1, blocks, SPAN, 2 * BLOCK), lambda r, p: (r, p, 0, 0, 0)),
            bias,
            bias,
        ],
        out_specs=[part(0)] * 3 + [pl.BlockSpec((1, 1, 4, 8, BLOCK), lambda r, p: (r, p, 0, 0, 0))],
        out_shape=[grads] * 3 + [jax.ShapeDtypeStruct((rows, pairs, 4, 8, BLOCK), F32)],
        scratch_shapes=[pltpu.VMEM((tokens + 2 * RADIUS, BLOCK), LOW)] * 2
        + [pltpu.VMEM((tokens + 2 * RADIUS, BLOCK), F32)] * 2,
        compiler_params=params(2),
        name="attention_backward",
    )(qkv, qkv, qkv, grad, probs, far, order)


TILE = 256
PARTS = 6


def block_kernel(
    att_ref, normed_ref, cot_ref, out_w_ref, up_ref, down_ref, gain_ref, shift_ref,
    result_ref, grad_two_ref, grad_att_ref, grad_out_ref, grad_up_ref, grad_down_ref, norms_ref,
    act_all, up_all, second_all, down_all, attn_all, att_all, slope_tile,
):
    step = pl.program_id(0)
    width = att_ref.shape[1]
    steps = act_all.shape[1] // TILE
    piece = act_all.shape[2]

    @pl.when(step == 0)
    def _():
        norms_ref[...] = jnp.zeros_like(norms_ref)

    @pl.when(step < steps)
    def _():
        at = pl.ds(pl.multiple_of(step * TILE, TILE), TILE)
        att = att_ref[...]
        att_all[at, :] = att
        resid = normed_ref[...] + nn(att, out_w_ref[...])
        unit_two, rstd_two = norm_parts(resid)
        gain_two, gain_three = gain_ref[1:2, :], gain_ref[2:3, :]
        normed = unit_two * gain_two + shift_ref[1:2, :]
        second = normed.astype(LOW)
        second_all[at, :] = second
        resid = normed
        for c in range(PARTS):
            cols = slice(c * piece, (c + 1) * piece)
            act, deriv = gelu_pair(nn(second, up_ref[:, cols]))
            slope_tile[:, cols] = deriv.astype(LOW)
            act = act.astype(LOW)
            act_all[c, at, :] = act
            resid = resid + nn(act, down_ref[cols, :])
        unit, rstd = norm_parts(resid)
        result_ref[...] = (unit * gain_three + shift_ref[2:3, :]).astype(LOW)
        cot = cot_ref[...].astype(F32)
        norms_ref[2] += fold(cot * unit)
        norms_ref[3] += fold(cot)
        grad = norm_back(cot, unit, rstd, gain_three)
        low = grad.astype(LOW)
        down_all[at, :] = low
        for c in range(PARTS):
            cols = slice(c * piece, (c + 1) * piece)
            up_low = (nt(low, down_ref[cols, :]) * slope_tile[:, cols].astype(F32)).astype(LOW)
            up_all[c, at, :] = up_low
            grad = grad + nt(up_low, up_ref[:, cols])
        norms_ref[0] += fold(grad * unit_two)
        norms_ref[1] += fold(grad)
        grad = norm_back(grad, unit_two, rstd_two, gain_two)
        grad_two_ref[...] = grad
        low = grad.astype(LOW)
        attn_all[at, :] = low
        grad_att_ref[...] = nt(low, out_w_ref[...]).astype(LOW)

    @pl.when(step >= steps)
    def _():
        c = step - steps
        grad_down_ref[...] = tn(act_all[c], down_all[...]).astype(LOW)
        grad_up_ref[...] = tn(second_all[...], up_all[c]).astype(LOW)
        cols = pl.ds(pl.multiple_of(c * BLOCK, BLOCK), BLOCK)
        grad_out_ref[...] = tn(att_all[:, cols], attn_all[...]).astype(LOW)


def block_both(att, normed, cot, out_w, up, down, gains, shifts):
    tokens, width = att.shape
    wide = up.shape[1]
    steps = tokens // TILE
    piece = wide // PARTS
    tile = lambda cols: pl.BlockSpec((TILE, cols), lambda s: (jnp.minimum(s, steps - 1), 0))
    late = lambda s: jnp.maximum(s - steps, 0)
    return pl.pallas_call(
        block_kernel,
        grid=(steps + PARTS,),
        in_specs=[
            tile(width), tile(width), tile(width),
            whole((width, width)), whole(up.shape), whole(down.shape), whole(gains.shape), whole(shifts.shape),
        ],
        out_specs=[
            tile(width), tile(width), tile(width),
            pl.BlockSpec((width // PARTS, width), lambda s: (late(s), 0)),
            pl.BlockSpec((width, piece), lambda s: (0, late(s))),
            pl.BlockSpec((piece, width), lambda s: (late(s), 0)),
            pl.BlockSpec((4, 8, width), lambda s: (0, 0, 0)),
        ],
        out_shape=[
            jax.ShapeDtypeStruct((tokens, width), LOW),
            jax.ShapeDtypeStruct((tokens, width), F32),
            jax.ShapeDtypeStruct((tokens, width), LOW),
            jax.ShapeDtypeStruct((width, width), LOW),
            jax.ShapeDtypeStruct(up.shape, LOW),
            jax.ShapeDtypeStruct(down.shape, LOW),
            jax.ShapeDtypeStruct((4, 8, width), F32),
        ],
        scratch_shapes=[
            pltpu.VMEM((PARTS, tokens, piece), LOW),
            pltpu.VMEM((PARTS, tokens, piece), LOW),
            pltpu.VMEM((tokens, width), LOW),
            pltpu.VMEM((tokens, width), LOW),
            pltpu.VMEM((tokens, width), LOW),
            pltpu.VMEM((tokens, width), LOW),
            pltpu.VMEM((TILE, wide), LOW),
        ],
        compiler_params=params(1),
        name="block_both",
    )(att, normed, cot, out_w, up, down, gains, shifts)


def graph_back_kernel(
    dq_ref, dk_ref, dv_ref, low_ref, two_ref, unit_ref, rstd_ref, slope_ref, hidden_ref, agg1_ref,
    agg2_ref, x_ref, adj_ref, cols_ref, graph_ref, qkv_w_ref, gain_ref,
    input_grad_ref, grad_qkv_ref, grad_graph_ref, norms_ref, edge_ref,
    branch_all, pre_all, one_row, mean_row, back_row,
):
    step = pl.program_id(0)
    rows, tokens, width = dq_ref.shape
    blocks = tokens // BLOCK
    chunk = 2 * BLOCK
    chunks = tokens // chunk

    @pl.when(step == 0)
    def _():
        norms_ref[...] = jnp.zeros_like(norms_ref)
        edge_ref[...] = jnp.zeros_like(edge_ref)

    def spread():
        back_row[...] = jnp.zeros_like(back_row)
        for b in range(blocks):
            back_row[b * BLOCK : b * BLOCK + WIDE, :] += nn(adj_ref[0, b], mean_row[b * BLOCK : (b + 1) * BLOCK, :])

    @pl.when(step < rows)
    def _():
        base = step * tokens
        for c in range(chunks):
            part = slice(c * chunk, (c + 1) * chunk)
            grad = two_ref[0, part, :]
            for k, ref in enumerate((dq_ref, dk_ref, dv_ref)):
                grad = grad + nt(ref[step, part, :], qkv_w_ref[:, k * width : (k + 1) * width])
            unit = unit_ref[0, part, :].astype(F32)
            norms_ref[0] += fold(grad * unit)
            norms_ref[1] += fold(grad)
            grad = norm_back(grad, unit, rstd_ref[0, part, :], gain_ref[0:1, :])
            one_row[part, :] = grad
            low = grad.astype(LOW)
            branch_all[pl.ds(pl.multiple_of(base + c * chunk, chunk), chunk), :] = low
            mean_row[part, :] = (nt(low, graph_ref[:, 3 * width : 4 * width]) * cols_ref[0, part, 2:3]).astype(LOW)
        spread()
        for c in range(chunks):
            part = slice(c * chunk, (c + 1) * chunk)
            at = pl.ds(pl.multiple_of(base + c * chunk, chunk), chunk)
            grad = back_row[REACH + c * chunk : REACH + (c + 1) * chunk, :]
            grad = grad + nt(branch_all[at, :], graph_ref[:, 2 * width : 3 * width])
            grad = grad * slope_ref[0, part, :].astype(F32)
            edge_ref[0] += fold(grad * cols_ref[0, part, 0:1])
            edge_ref[1] += fold(grad * cols_ref[0, part, 1:2])
            low = grad.astype(LOW)
            pre_all[at, :] = low
            mean_row[part, :] = (nt(low, graph_ref[:, width : 2 * width]) * cols_ref[0, part, 2:3]).astype(LOW)
        spread()
        for c in range(chunks):
            part = slice(c * chunk, (c + 1) * chunk)
            at = pl.ds(pl.multiple_of(base + c * chunk, chunk), chunk)
            grad = one_row[part, :] + back_row[REACH + c * chunk : REACH + (c + 1) * chunk, :]
            input_grad_ref[0, part, :] = grad + nt(pre_all[at, :], graph_ref[:, 0:width])

    flat = lambda ref: ref[...].reshape(rows * tokens, width)
    for k, (left, right) in enumerate(
        ((low_ref, dq_ref), (low_ref, dk_ref), (low_ref, dv_ref))
    ):
        @pl.when(step == rows + k)
        def _(left=left, right=right):
            grad_qkv_ref[...] = tn(flat(left), flat(right)).astype(LOW)

    for k, (left, right) in enumerate(
        ((x_ref, pre_all), (agg1_ref, pre_all), (hidden_ref, branch_all), (agg2_ref, branch_all))
    ):
        @pl.when(step == rows + 3 + k)
        def _(left=left, right=right):
            grad_graph_ref[...] = tn(flat(left), right[...]).astype(LOW)


def graph_backward(dq, dk, dv, low, two, unit, rstd, slope, hidden, agg1, agg2, x, adj, cols, graph_w, qkv_w, gains):
    rows, tokens, width = x.shape
    blocks = tokens // BLOCK
    per_row = lambda *shape: pl.BlockSpec(
        (1,) + shape, lambda s: (jnp.minimum(s, rows - 1),) + (0,) * len(shape)
    )
    full = whole((rows, tokens, width))
    return pl.pallas_call(
        graph_back_kernel,
        grid=(rows + 7,),
        in_specs=[
            full, full, full, full,
            per_row(tokens, width), per_row(tokens, width), per_row(tokens, 1), per_row(tokens, width),
            full, full, full, full,
            per_row(blocks, WIDE, BLOCK), per_row(tokens, 8),
            whole(graph_w.shape), whole(qkv_w.shape), whole(gains.shape),
        ],
        out_specs=[
            per_row(tokens, width),
            pl.BlockSpec((width, width), lambda s: (0, jnp.clip(s - rows, 0, 2))),
            pl.BlockSpec((width, width), lambda s: (0, jnp.clip(s - rows - 3, 0, 3))),
            pl.BlockSpec((2, 8, width), lambda s: (0, 0, 0)),
            pl.BlockSpec((2, 8, width), lambda s: (0, 0, 0)),
        ],
        out_shape=[
            jax.ShapeDtypeStruct((rows, tokens, width), F32),
            jax.ShapeDtypeStruct((width, 3 * width), LOW),
            jax.ShapeDtypeStruct((width, 4 * width), LOW),
            jax.ShapeDtypeStruct((2, 8, width), F32),
            jax.ShapeDtypeStruct((2, 8, width), F32),
        ],
        scratch_shapes=[
            pltpu.VMEM((rows * tokens, width), LOW),
            pltpu.VMEM((rows * tokens, width), LOW),
            pltpu.VMEM((tokens, width), F32),
            pltpu.VMEM((tokens, width), LOW),
            pltpu.VMEM((tokens + 2 * REACH, width), F32),
        ],
        compiler_params=params(1),
        name="graph_backward",
    )(dq, dk, dv, low, two, unit, rstd, slope, hidden, agg1, agg2, x, adj, cols, graph_w, qkv_w, gains)


def device_work(inputs, coords, neighbours, counts, doc_length, graph_w, qkv_w, out_w, up, down,
                edge_proj, norm_gains, norm_shifts, distance_rate, order_rate, cotangent):
    rows, tokens, width = inputs.shape
    length = doc_length[:, 0]
    (adj, cols, agg1, slope, hidden, agg2, unit, rstd, normed, low, qkv) = graph_forward(
        length, neighbours, counts[:, None, :], coords, inputs, graph_w, edge_proj, norm_gains, norm_shifts, qkv_w
    )
    att, probs, far, order = attention_forward(length, distance_rate, order_rate, coords, qkv)
    flat = lambda v: v.reshape(rows * tokens, width)
    tall = lambda v: v.reshape(rows, tokens, width)
    result, two, grad_att, grad_out, grad_up, grad_down, norms_late = block_both(
        flat(att), flat(normed), flat(cotangent), out_w, up, down, norm_gains, norm_shifts
    )
    dq, dk, dv, rates = attention_backward(qkv, tall(grad_att), probs, far, order)
    input_grad, grad_qkv, grad_graph, norms_first, edge = graph_backward(
        dq, dk, dv, low, tall(two), unit, rstd, slope, hidden, agg1, agg2, inputs, adj, cols, graph_w, qkv_w, norm_gains
    )
    norms = jnp.concatenate([norms_first, norms_late], axis=0).sum(axis=1)
    rates = rates.sum(axis=(0, 3, 4)).reshape(-1, 2, 2)
    small = (edge.sum(axis=1), norms[0::2], norms[1::2], rates[:, :, 0].reshape(-1), rates[:, :, 1].reshape(-1))
    return tall(result), input_grad, grad_graph, grad_qkv, grad_out, grad_up, grad_down, small


def add_small(small, axes):
    edge, gains, shifts, rates, orders = small
    width = edge.shape[1]
    heads = rates.shape[0]
    line = jnp.concatenate([rates, orders, jnp.zeros((width - 2 * heads,), F32)])[None]
    total = lax.psum(jnp.concatenate([edge, gains, shifts, line], axis=0), axes)
    return total[0:2], total[2:5], total[5:8], total[8, :heads], total[8, heads : 2 * heads]


def local(
    inputs, coords, neighbours, counts, doc_length, self_one, near_one, self_two, near_two, edge_proj,
    qkv_proj, out_proj, up_proj, down_proj, norm_gains, norm_shifts, distance_rate, order_rate, cotangent,
):
    axes = ("wide", "narrow")
    width = inputs.shape[2]
    gather = lambda v: lax.all_gather(v, axes, axis=0, tiled=True)
    scatter = lambda v: lax.psum_scatter(v, axes, scatter_dimension=0, tiled=True)
    graph_w = gather(jnp.concatenate([self_one, near_one, self_two, near_two], axis=1))
    qkv_out = gather(jnp.concatenate([qkv_proj, out_proj], axis=1))
    up, down = gather(up_proj), gather(down_proj)
    result, input_grad, grad_graph, grad_qkv, grad_out, grad_up, grad_down, small = device_work(
        inputs, coords, neighbours, counts, doc_length, graph_w, qkv_out[:, : 3 * width], qkv_out[:, 3 * width :],
        up, down, edge_proj, norm_gains, norm_shifts, distance_rate, order_rate, cotangent,
    )
    down_own = scatter(grad_down).astype(F32)
    up_own = scatter(jnp.concatenate([grad_up, grad_out], axis=1)).astype(F32)
    rest = scatter(jnp.concatenate([grad_graph, grad_qkv], axis=1)).astype(F32)
    edge, gains, shifts, rates, orders = add_small(small, axes)
    wide = up_proj.shape[1]
    return (
        result, input_grad,
        rest[:, :width], rest[:, width : 2 * width], rest[:, 2 * width : 3 * width], rest[:, 3 * width : 4 * width],
        edge,
        rest[:, 4 * width :], up_own[:, wide:], up_own[:, :wide], down_own,
        gains, shifts, rates, orders,
    )


def solution(mesh):
    axes = ("wide", "narrow")
    middle, last = P(None, axes, None), P(None, None, axes)
    count, weight, same = P(None, axes), P(axes, None), P()
    return jax.shard_map(
        local,
        mesh=mesh,
        in_specs=(middle, last, last, count, count)
        + (weight,) * 4
        + (same,)
        + (weight,) * 4
        + (same,) * 4
        + (middle,),
        out_specs=(middle, middle) + (weight,) * 4 + (same,) + (weight,) * 4 + (same,) * 4,
        check_vma=False,
    )
```

time: 2100 us -> 735 us (0.35)
  matrix products: 720 us -> 0 us
  local copies, waits for them, and re-layouts: 335 us -> 18.2 us
  other arithmetic: 317 us -> 17.4 us
  Pallas kernels: 0 us -> 242 us
  waiting for transfers between devices: 632 us -> 392 us
    dot_general x226 -> x0, matrix products: 720 us -> none  [the longest x84 358 us: dot_right_t(): lax.dot_general(left, right, (((1,), (1,)), ((), ())), preferred_element_...]
    reduce_scatter x7 -> x3, waiting for transfers between devices: 523 us -> 199 us  [local(): lax.psum_scatter(v, axes, scatter_dimension=0, tiled=True)]
    pallas_call x0 -> x5, Pallas kernels: none -> 242 us  [the longest x1 79.3 us: block_both(): pl.pallas_call(block_kernel, grid=(steps + PARTS,), in_specs=[tile(width)...]
    dynamic_slice x280 -> x0, local copies, waits for them, and re-layouts: 197 us -> none  [the longest x96 119 us: attention_forward(): lax.map(one_head, (per_head, distance_rate, order_rate))]
    all_gather x8 -> x4, waiting for transfers between devices: 0.01 us -> 192 us  [local(): gather = lambda v: lax.all_gather(v, axes, axis=0, tiled=True)]
    add x108 -> x0, other arithmetic: 178 us -> none  [the longest x80 178 us: add_slot(): return total + hit.astype(jnp.float32)]
    unnamed x17 -> x7, waiting for transfers between devices: 109 us -> 1.29 us
    reduce_sum x61 -> x3, other arithmetic: 106 us -> 0.19 us  [the longest x1 0.12 us: device_work(): rates = rates.sum(axis=(0, 3, 4)).reshape(-1, 2, 2)]
  transfers between devices with their start and end apart: 16 -> 7, of which waited for: 6 -> 5; matrix products, arithmetic and copies ran while one was open for 61% -> 4% of each run, Pallas kernels for 0% -> 22%
where the time goes in v1:
time: 735 us; the launch traced here: 725 us
  waiting for transfers between devices  392 us (53%)
  Pallas kernels  242 us (33%)
  blocking collectives  40.1 us (5%)
  local copies, waits for them, and re-layouts  18.2 us (2%)
  other arithmetic  17.4 us (2%)
  between operations  14.4 us (2%)
    reduce_scatter x3, waiting for transfers between devices, local(): lax.psum_scatter(v, axes, scatter_dimension=0, tiled=True)  199 us
    all_gather x4, waiting for transfers between devices, local(): gather = lambda v: lax.all_gather(v, axes, axis=0, tiled=True)  192 us
    pallas_call x1, Pallas kernels, block_both(): pl.pallas_call(block_kernel, grid=(steps + PARTS,), in_specs=[tile(width)...  79.3 us
    pallas_call x1, Pallas kernels, graph_backward(): pl.pallas_call(graph_back_kernel, grid=(rows + 7,), in_specs=[full, full,...  63.3 us
    psum x1, blocking collectives, add_small(): total = lax.psum(jnp.concatenate([edge, gains, shifts, line], axis=0), axes)  40.1 us
    pallas_call x1, Pallas kernels, attention_backward(): pl.pallas_call(attention_back_kernel, grid=(rows, pairs), in_specs=[part(...  36.4 us
    pallas_call x1, Pallas kernels, graph_forward(): pl.pallas_call(graph_kernel, grid=(rows,), in_specs=[pl.BlockSpec(memory_...  35.1 us
    pallas_call x1, Pallas kernels, attention_forward(): pl.pallas_call(attention_kernel, grid=(rows, pairs), in_specs=[smem, smem...  28.2 us
  transfers between devices with their start and end apart: 7, of which 5 were waited for; matrix products, arithmetic and copies ran while one was open for 4% of the time, Pallas kernels for 22%

profile of v1, /device:TPU:0, one launch (start us, length us, event | category | flops | bytes accessed | tf_op | source)
XLA Modules:
  0.0 724.7 jit_solution(5635406401480801301)
XLA Ops:
  7.2 0.0 all-gather.7.cloned.1.call-start
  7.2 1.6 pad_maximum_fusion.3
  8.8 0.0 all-gather.5.cloned.1.call-start
  8.9 1.5 pad_maximum_fusion.2
  10.4 0.0 all-gather.5.cloned.1.call-update
  10.4 0.0 all-gather.11.cloned.1.call-start
  10.5 0.7 all-gather.11.cloned.1.call-update
  11.2 0.0 all-gather.9.cloned.1.call-start
  11.2 0.5 all-gather.9.cloned.1.call-update
  11.7 0.0 reduce-scatter.8.cloned.1.call-start
  11.8 1.3 broadcast_in_dim.9.count_ref
  13.1 64.8 %all-gather.7.cloned.1.call-done = bf16[768,3072]{1,0:T(8,128)(2,1)} async-done(((bf16[24,3072]{1,0:T(8,128)(2,1)}), bf16[768,3072]{1,0:T(8,128)(2,1)}) %all-gather.7.cloned.1.call-update) | async-done | bytes 4718608 | tf_op jit(solution)/shard_map/all_gather | solution.py:647
  77.9 4.1 slice.72.qkv_w_ref
  81.9 61.9 %all-gather.5.cloned.1.call-done.graph_ref = bf16[768,3072]{1,0:T(8,128)(2,1)} async-done(((bf16[24,3072]{1,0:T(8,128)(2,1)}), bf16[768,3072]{1,0:T(8,128)(2,1)}) %all-gather.5.cloned.1.call-update) | async-done | bytes 4718608 | tf_op jit(solution)/shard_map/all_gather | solution.py:647
  143.8 35.1 %graph_forward.1 = (bf16[2,6,256,128]{3,2,1,0:T(8,128)(2,1)}, f32[2,768,8]{2,1,0:T(8,128)}, bf16[2,768,768]{2,1,0:T(8,128)(2,1)}, bf16[2,768,768]{2,1,0:T(8,128)...) custom-call(s32[2]{0:T(128)} %bitcast.22, ...), custom_call_target="tpu_custom_call" | custom-call | tf_op jit(solution)/shard_map/graph_forward/pallas_call | solution.py:161
  179.0 28.2 %attention_forward.1 = (bf16[2,768,768]{2,1,0:T(8,128)(2,1)}, bf16[2,6,6,384,256]{4,3,2,1,0:T(8,128)(2,1)}, f32[2,6,384,128]{3,2,1,0:T(8,128)}, f32[2,6,384,128]{3,2,1,0:T(8,128)}) custom-call(s32[2]{0:T(128)} %bitcast.23, f32[12]{0:T(128)} %dist_rate_ref.1, f32[12]{0:T(128)} %order_rate_ref.1, f32[2,2,768]{2,1,0:T(2,128)} %point_ref.3, ...), custom_call_target="tpu_custom_call" | custom-call | tf_op jit(solution)/shard_map/attention_forward/pallas_call | solution.py:292
  207.1 2.4 slice.73.out_w_ref
  209.5 65.0 %all-gather.9.cloned.1.call-done.up_ref = bf16[768,3072]{1,0:T(8,128)(2,1)} async-done(((bf16[24,3072]{1,0:T(8,128)(2,1)}), bf16[768,3072]{1,0:T(8,128)(2,1)}) %all-gather.9.cloned.1.call-update) | async-done | bytes 4718608 | tf_op jit(solution)/shard_map/all_gather | solution.py:647
  274.5 79.3 %block_both.1 = (bf16[1536,768]{1,0:T(8,128)(2,1)}, f32[1536,768]{1,0:T(8,128)}, bf16[1536,768]{1,0:T(8,128)(2,1)}, bf16[768,768]{1,0:T(8,128)(2,1)}, bf16[768,3...) custom-call(bf16[1536,768]{1,0:T(8,128)(2,1)} %bitcast.19, f32[1536,768]{1,0:T(8,128)} %bitcast.17, ...), custom_call_target="tpu_custom_call" | custom-call | tf_op jit(solution)/shard_map/block_both/pallas_call | solution.py:456
  353.9 0.0 reduce-scatter.8.cloned.1.call-update
  353.9 0.0 reduce-scatter.6.cloned.1.call-start
  353.9 1.2 copy-done
  355.1 5.3 pad_maximum_fusion.1
  360.4 0.0 reduce-scatter.6.cloned.1.call-update
  360.4 0.0 reduce-scatter.4.cloned.1.call-start
  360.5 36.4 %attention_backward.1 = (bf16[2,768,768]{2,1,0:T(8,128)(2,1)}, bf16[2,768,768]{2,1,0:T(8,128)(2,1)}, bf16[2,768,768]{2,1,0:T(8,128)(2,1)}, f32[2,6,4,8,128]{4,3,2,1,0:T(8,128)}) custom-call(bf16[2,768,2304]{2,1,0:T(8,128)(2,1)} %get-tuple-element.46.q_ref.k_ref.v_ref, bf16[2,768,2304]{2,1,0:T(8,128)(2,1)} %get-tuple-element.46.q_ref.k_ref.v_ref, ...), custom_call_target="tpu_custom_call" | custom-call | tf_op jit(solution)/shard_map/attention_backward/pallas_call | solution.py:361
  396.8 63.3 %graph_backward.1 = (f32[2,768,768]{2,1,0:T(8,128)}, bf16[768,2304]{1,0:T(8,128)(2,1)}, bf16[768,3072]{1,0:T(8,128)(2,1)}, f32[2,8,768]{2,1,0:T(8,128)}, f32[2,8,768]{2,1,0:T(8,128)}) custom-call(bf16[2,768,768]{2,1,0:T(8,128)(2,1)} %get-tuple-element.54.dq_ref, bf16[2,768,768]{2,1,0:T(8,128)(2,1)} %get-tuple-element.55.dk_ref, ...), custom_call_target="tpu_custom_call" | custom-call | tf_op jit(solution)/shard_map/graph_backward/pallas_call | solution.py:573
  460.1 7.1 pad_maximum_fusion
  467.3 0.0 reduce-scatter.4.cloned.1.call-update
  467.3 0.9 copy-done.2
  468.3 0.1 reduce_sum.29
  468.4 0.1 copy.38
  468.5 0.1 copy.39
  468.6 0.1 reshape_squeeze.6
  468.7 0.1 copy.40
  468.7 0.1 reshape_squeeze.7
  468.8 0.1 pad_maximum_fusion.5
  469.0 40.1 %psum.7 = f32[9,768]{1,0:T(8,128)S(1)} all-reduce(f32[9,768]{1,0:T(8,128)S(1)} %pad_maximum_fusion.4), channel_id=1, replica_groups=mesh['wide'=16,'narrow'=2] {'wide','narrow'}, use_global_device_ids=true, to_apply=%region_4.0 | all-reduce | flops 6912 | bytes 55296 | tf_op jit(solution)/shard_map/psum | solution.py:637
  509.0 0.6 slice.80
  509.6 0.6 slice_bitcast_fusion
  510.2 0.6 fusion.1
  510.8 1.6 convert_element_type.11
  512.5 65.7 %reduce-scatter.6.cloned.1.call-done = bf16[24,3840]{1,0:T(8,128)(2,1)} async-done(((bf16[768,3840]{1,0:T(8,128)(2,1)}), bf16[24,3840]{1,0:T(8,128)(2,1)}) %reduce-scatter.6.cloned.1.call-update) | async-done | bytes 184336 | tf_op jit(solution)/shard_map/reduce_scatter | solution.py:648
  578.2 1.6 slice.83
  579.8 1.4 slice.82
  581.2 133.3 %reduce-scatter.4.cloned.1.call-done = bf16[24,5376]{1,0:T(8,128)(2,1)} async-done(((bf16[768,5376]{1,0:T(8,128)(2,1)}), bf16[24,5376]{1,0:T(8,128)(2,1)}) %reduce-scatter.4.cloned.1.call-update) | async-done | bytes 258064 | tf_op jit(solution)/shard_map/reduce_scatter | solution.py:648
  714.5 1.5 fusion
  716.0 1.6 slice.81
  (19 shorter events, 0.2 us)
Async XLA Ops:
  7.2 70.7 %all-gather.7.cloned.1.call-start = ((), (), s32[]{:S(2)}) async-start(), calls=%async_computation.4 | async-start | bytes 4866048 | tf_op jit(solution)/shard_map/all_gather | solution.py:647
  8.8 135.0 %all-gather.5.cloned.1.call-start = ((), (), s32[]{:S(2)}) async-start(), calls=%async_computation.3 | async-start | bytes 4866048 | tf_op jit(solution)/shard_map/all_gather | solution.py:647
  10.4 199.1 %all-gather.11.cloned.1.call-start = ((), (), s32[]{:S(2)}) async-start(), calls=%async_computation.6 | async-start | bytes 4866048 | tf_op jit(solution)/shard_map/all_gather | solution.py:647
  11.2 263.4 %all-gather.9.cloned.1.call-start = ((), (), s32[]{:S(2)}) async-start(), calls=%async_computation.5 | async-start | bytes 4866048 | tf_op jit(solution)/shard_map/all_gather | solution.py:647
  11.7 499.1 %reduce-scatter.8.cloned.1.call-start = ((), (), s32[]{:S(2)}) async-start(), calls=%async_computation.9 | async-start | bytes 4866048 | tf_op jit(solution)/shard_map/reduce_scatter | solution.py:648
  353.9 1.3 copy-start
  353.9 224.3 %reduce-scatter.6.cloned.1.call-start = ((), (), s32[]{:S(2)}) async-start(), calls=%async_computation.8 | async-start | bytes 6082560 | tf_op jit(solution)/shard_map/reduce_scatter | solution.py:648
  360.4 354.1 %reduce-scatter.4.cloned.1.call-start = ((), (), s32[]{:S(2)}) async-start(), calls=%async_computation.7 | async-start | bytes 8515584 | tf_op jit(solution)/shard_map/reduce_scatter | solution.py:648
  467.3 0.9 copy-start.2
  467.3 0.9 copy-start.4
  467.3 1.0 copy-start.1
  467.3 1.7 copy-start.3
Sparse Core Ops, SparseCore 0:
  11.5 66.3 all-gather.6
  81.4 62.4 all-gather.4
  146.8 62.4 all-gather.10
  212.0 62.4 all-gather.8
  354.0 105.7 reduce-scatter.7
  466.3 111.8 reduce-scatter.5
  585.1 129.4 reduce-scatter.3

commit v2 on v1

v2 whole, which is shorter than its diff:
```python
import functools
import jax
import jax.numpy as jnp
from jax import lax
from jax.experimental import pallas as pl
from jax.experimental.pallas import tpu as pltpu
from jax.sharding import PartitionSpec as P

RADIUS = 128
REACH = 64
BLOCK = 128
WIDE = BLOCK + 2 * REACH
SPAN = BLOCK + 2 * RADIUS
FAR = 1e10
F32 = jnp.float32
LOW = jnp.bfloat16
VMEM = 60 * 2**20


def dot(left, right, dims):
    return lax.dot_general(left, right, ((dims[:1], dims[1:]), ((), ())), preferred_element_type=F32)


def nn(left, right):
    return dot(left, right, (1, 0))


def nt(left, right):
    return dot(left, right, (1, 1))


def tn(left, right):
    return dot(left, right, (0, 0))


def gelu_pair(pre):
    slope = 0.7978845608028654
    square = pre * pre
    half = 0.5 + 0.5 * jnp.tanh(pre * (slope + (slope * 0.044715) * square))
    act = pre * half
    deriv = half + act * (1.0 - half) * (2.0 * slope + (6.0 * slope * 0.044715) * square)
    return act, deriv


def norm_parts(values):
    centre = values - jnp.mean(values, axis=-1, keepdims=True)
    rstd = lax.rsqrt(jnp.mean(centre * centre, axis=-1, keepdims=True) + 1e-05)
    return centre * rstd, rstd


def norm_back(grad, unit, rstd, gain):
    scaled = grad * gain
    mean = jnp.mean(scaled, axis=-1, keepdims=True)
    along = jnp.mean(scaled * unit, axis=-1, keepdims=True)
    return rstd * (scaled - mean - unit * along)


def fold(values):
    rows, cols = values.shape
    return jnp.sum(values.reshape(rows // 8, 8, cols), axis=0)


def whole(shape, space=None):
    return pl.BlockSpec(shape, lambda *_: (0,) * len(shape), pipeline_mode=pl.Buffered(1))


def params(grid_rank, **more):
    return pltpu.CompilerParams(
        vmem_limit_bytes=VMEM, dimension_semantics=("arbitrary",) * grid_rank, **more
    )


def fill_bias(length, point_ref, far_ref, order_ref, row):
    tokens = point_ref.shape[2]
    side = jnp.zeros((2, RADIUS), F32)
    padded = jnp.concatenate([side, point_ref[row], side], axis=1)
    tall = jnp.concatenate([padded, jnp.zeros((6, tokens + 2 * RADIUS), F32)], axis=0)
    for b in range(tokens // BLOCK):
        window = tall[:, b * BLOCK : b * BLOCK + SPAN].T
        key_x, key_y = window[:, 0:1], window[:, 1:2]
        lanes = slice(b * BLOCK, (b + 1) * BLOCK)
        delta_x = key_x - point_ref[row, 0:1, lanes]
        delta_y = key_y - point_ref[row, 1:2, lanes]
        dist = jnp.log(1.0 + 16.0 * (delta_x * delta_x + delta_y * delta_y))
        query = lax.broadcasted_iota(jnp.int32, (SPAN, BLOCK), 1) + b * BLOCK
        key = lax.broadcasted_iota(jnp.int32, (SPAN, BLOCK), 0) + (b * BLOCK - RADIUS)
        allowed = (jnp.abs(query - key) <= RADIUS) & ((query >= length) == (key >= length))
        allowed = allowed & (key >= 0) & (key < tokens)
        far_ref[row, b] = jnp.where(allowed, dist, FAR)
        order_ref[row, b] = jnp.tanh(4.0 * delta_x)


def pair_rows(values):
    lane = lax.broadcasted_iota(jnp.int32, values.shape, 1)
    zero = jnp.zeros_like(values)
    first = jnp.where(lane < BLOCK // 2, values, zero)
    second = jnp.where(lane < BLOCK // 2, zero, values)
    return jnp.concatenate([first, second], axis=0)


def pair_pick(values):
    lane = lax.broadcasted_iota(jnp.int32, (BLOCK, BLOCK), 1)
    return jnp.where(lane < BLOCK // 2, values[:BLOCK], values[BLOCK:])


def pad_rows(pad_ref, values):
    tokens = values.shape[0]
    zeros = jnp.zeros((RADIUS, values.shape[1]), pad_ref.dtype)
    pad_ref[pl.ds(0, RADIUS), :] = zeros
    pad_ref[pl.ds(RADIUS + tokens, RADIUS), :] = zeros
    pad_ref[pl.ds(RADIUS, tokens), :] = values


FIRST, OWN, PASSED, SIBLING = 0, 1, 2, 3


class Place:
    def __init__(self, depth):
        self.depth = depth
        wide, self.x = lax.axis_index("wide"), lax.axis_index("narrow")
        self.core = lax.rem(wide, 2)
        self.y = lax.rem(lax.div(wide, 2), 2)
        self.z = lax.div(wide, 4)
        core, y, x = self.core, self.y, self.x
        self.first_y = (1 - core) * (1 - y) + core * y
        self.first_x = core * (1 - x) + (1 - core) * x
        self.second_y = core * (1 - y) + (1 - core) * y
        self.second_x = (1 - core) * (1 - x) + core * x

    def at(self, z, y, core, x):
        return ((z * 2 + y) * 2 + core, x)

    def along(self, k):
        return lax.rem(self.z + k, self.depth)

    def partners(self):
        along = [self.at(self.along(k), self.y, self.core, self.x) for k in range(1, self.depth)]
        return along + [
            self.at(self.z, self.first_y, self.core, self.first_x),
            self.at(self.z, self.second_y, self.core, self.second_x),
            self.at(self.z, self.y, 1 - self.core, self.x),
        ]


def meet(place):
    barrier = pltpu.get_barrier_semaphore()
    partners = place.partners()
    for partner in partners:
        pl.semaphore_signal(barrier, inc=1, device_id=partner, device_id_type=pl.DeviceIdType.MESH)
    pl.semaphore_wait(barrier, len(partners))


class Gather:
    def __init__(self, place, land, send, recv, group):
        self.place, self.land, self.send, self.recv, self.group = place, land, send, recv, group

    def copy(self, view, slot, device):
        return pltpu.make_async_remote_copy(
            src_ref=view, dst_ref=view, send_sem=self.send.at[self.group, slot], recv_sem=self.recv.at[self.group, slot],
            device_id=device, device_id_type=pl.DeviceIdType.MESH,
        )

    def pieces(self, stage):
        p, land = self.place, self.land
        base = p.depth - 1
        mine = land.at[:, p.y, p.core, p.x]
        if stage == "along":
            here = land.at[p.z, p.y, p.core, p.x]
            found = []
            for k in range(1, p.depth):
                there = land.at[p.along(p.depth - k), p.y, p.core, p.x]
                found.append((here, there, k - 1, p.at(p.along(k), p.y, p.core, p.x)))
            return found
        first = p.at(p.z, p.first_y, p.core, p.first_x)
        second = p.at(p.z, p.second_y, p.core, p.second_x)
        if stage == FIRST:
            return [(mine, land.at[:, p.first_y, p.core, p.first_x], base, first)]
        if stage == OWN:
            return [(mine, land.at[:, p.second_y, p.core, p.second_x], base + 1, second)]
        if stage == PASSED:
            return [(land.at[:, p.first_y, p.core, p.first_x], land.at[:, 1 - p.y, p.core, 1 - p.x], base + 2, second)]
        return [(land.at[:, :, p.core], land.at[:, :, 1 - p.core], base + 3, p.at(p.z, p.y, 1 - p.core, p.x))]

    def start(self, *stages):
        for stage in stages:
            for leaves, _, slot, device in self.pieces(stage):
                self.copy(leaves, slot, device).start()

    def arrive(self, *stages):
        for stage in stages:
            for _, arrives, slot, device in self.pieces(stage):
                self.copy(arrives, slot, device).wait_recv()

    def sent(self):
        for stage in ("along", FIRST, OWN, PASSED, SIBLING):
            for leaves, _, slot, device in self.pieces(stage):
                self.copy(leaves, slot, device).wait_send()


def merge_rows(full, land):
    depth, rows = land.shape[0], land.shape[4]

    @pl.loop(0, depth * 4)
    def _(k):
        z, y, core = lax.div(k, 4), lax.rem(lax.div(k, 2), 2), lax.rem(k, 2)
        pair = jnp.concatenate([land[z, y, core, 0].astype(F32), land[z, y, core, 1].astype(F32)], axis=0)
        full[pl.ds(pl.multiple_of(k * 2 * rows, 16), 2 * rows), :] = pair.astype(LOW)


def front_kernel(remote, *refs):
    (length_ref, dist_rate_ref, order_rate_ref, near_ref, count_ref, point_ref, x_ref, edge_w_ref, gain_ref, shift_ref,
     self1_ref, near1_ref, self2_ref, near2_ref, qkv_w_ref) = refs[:15]
    refs = refs[15:]
    shards, refs = (refs[:3], refs[3:]) if remote else ((), refs)
    outs, refs = refs[:18], refs[18:]
    fulls, refs = (refs[:3], refs[3:]) if remote else ((), refs)
    (adj, cols, agg1, slope, hidden, agg2, unit, rstd, normed, low, qkv, att, probs, far, order,
     first_w, second_w, third_w, pad, point_pad, rel, keys, values, out_sem, probs_sem, in_sem) = refs[:26]
    rows, slots, tokens = near_ref.shape
    width = x_ref.shape[2]
    pairs = width // BLOCK
    blocks = tokens // BLOCK
    chunk = 2 * BLOCK

    writes = {}

    def write(k, source, dest=None):
        writes[k] = pltpu.make_async_copy(source, outs[k] if dest is None else dest, out_sem.at[k])
        writes[k].start()

    if remote:
        land_a, land_b, land_q, send, recv = refs[26:]
        place = Place(land_a.shape[0])
        lands = (land_a, land_b, land_q) + tuple(fulls)
        groups = [Gather(place, land, send, recv, g) for g, land in enumerate(lands)]
        ga, gb, gq, go, gu, gd = groups
        column = lambda land, k: land.at[place.z, place.y, place.core, place.x, :, pl.ds(k * width, width)]
        own = lambda land: land.at[place.z, place.y, place.core, place.x]
        loads = [
            [pltpu.make_async_copy(ref, column(land_a, k), in_sem.at[k]) for k, ref in enumerate((self1_ref, near1_ref))],
            [pltpu.make_async_copy(ref, column(land_b, k), in_sem.at[2 + k]) for k, ref in enumerate((self2_ref, near2_ref))],
            [pltpu.make_async_copy(qkv_w_ref, own(land_q), in_sem.at[4])],
        ] + [[pltpu.make_async_copy(ref, own(full), in_sem.at[5 + k])] for k, (ref, full) in enumerate(zip(shards, fulls))]
        for load in loads:
            for copy in load:
                copy.start()
        meet(place)

        def begin(g):
            for copy in loads[g]:
                copy.wait()
            groups[g].start("along")

        begin(0)
        begin(1)
    else:
        loads = [
            pltpu.make_async_copy(ref, dest, in_sem.at[k])
            for k, (ref, dest) in enumerate((
                (self1_ref, first_w.at[:, pl.ds(0, width)]), (near1_ref, first_w.at[:, pl.ds(width, width)]),
                (self2_ref, second_w.at[:, pl.ds(0, width)]), (near2_ref, second_w.at[:, pl.ds(width, width)]),
                (qkv_w_ref, third_w),
            ))
        ]
        for copy in loads:
            copy.start()

    side = jnp.zeros((REACH, width), LOW)
    pad[pl.ds(0, REACH), :] = side
    pad[pl.ds(tokens + REACH, REACH), :] = side

    @pl.loop(0, rows)
    def _(row):
        length = length_ref[row]
        pad[pl.ds(REACH, tokens), :] = x_ref[row]
        points = point_ref[row]
        high = points.astype(LOW).astype(F32)
        mid = (points - high).astype(LOW).astype(F32)
        tail = points - high - mid
        split = jnp.concatenate([high, mid, tail, jnp.ones((1, tokens), F32), jnp.zeros((9, tokens), F32)], axis=0)
        edge_side = jnp.zeros((16, REACH), F32)
        point_pad[...] = jnp.concatenate([edge_side, split, edge_side], axis=1).astype(LOW)

        @pl.loop(0, blocks)
        def _(b):
            start = pl.multiple_of(b * BLOCK, BLOCK)
            lanes = pl.ds(start, BLOCK)
            near = near_ref[row, :, lanes]
            count = count_ref[row, :, lanes]
            spot = lax.broadcasted_iota(jnp.int32, (1, BLOCK), 1) + start
            slot = lax.broadcasted_iota(jnp.int32, (slots, BLOCK), 0)
            same = (near >= length) == (spot >= length)
            rel[...] = jnp.where((slot < count) & same, near - (start - REACH), -1)
            target = lax.broadcasted_iota(jnp.int32, (WIDE, BLOCK), 0)
            total = jnp.zeros((WIDE, BLOCK), F32)
            for s in range(slots):
                total = total + jnp.where(rel[s : s + 1, :] == target, 1.0, 0.0)
            band = total.astype(LOW)
            adj[row, b] = band
            sums = nn(point_pad[:, pl.ds(start, WIDE)], band)
            inverse = 1.0 / count.astype(F32)
            here = point_ref[row, :, lanes]
            edge = (sums[0:2] + sums[2:4] + sums[4:6] - sums[6:7] * here) * inverse
            lines = jnp.concatenate([edge, inverse, jnp.zeros((5, BLOCK), F32)], axis=0).T
            cols[row, lanes, :] = lines
            agg = tn(band, pad[pl.ds(start, WIDE), :])
            agg1[row, lanes, :] = (agg * lines[:, 2:3]).astype(LOW)

        if remote:
            @pl.when(row == 0)
            def _():
                ga.arrive("along")
                ga.start(FIRST, OWN)
                begin(2)

    write(0, adj)
    write(1, cols)
    write(2, agg1)
    if remote:
        ga.arrive(FIRST)
        ga.start(PASSED)
        gb.arrive("along")
        gb.start(FIRST, OWN)

    @pl.loop(0, rows)
    def _(row):
        fill_bias(length_ref[row], point_ref, far, order, row)

    write(13, far)
    write(14, order)
    if remote:
        ga.arrive(OWN, PASSED)
        ga.start(SIBLING)
        gb.arrive(FIRST)
        gb.start(PASSED)
        gq.arrive("along")
        gq.start(FIRST, OWN)
        begin(3)
        begin(4)
        ga.arrive(SIBLING)
        merge_rows(first_w, land_a)
    else:
        for copy in loads:
            copy.wait()
        write(16, second_w)
        write(17, third_w)
    write(15, first_w)

    @pl.loop(0, rows)
    def _(row):
        for c in range(tokens // chunk):
            part = slice(c * chunk, (c + 1) * chunk)
            pre = nn(x_ref[row, part, :], first_w[:, 0:width])
            pre = pre + nn(agg1[row, part, :], first_w[:, width : 2 * width])
            pre = pre + cols[row, part, 0:1] * edge_w_ref[0:1, :] + cols[row, part, 1:2] * edge_w_ref[1:2, :]
            act, deriv = gelu_pair(pre)
            slope[row, part, :] = deriv.astype(LOW)
            hidden[row, part, :] = act.astype(LOW)
            pad[REACH + c * chunk : REACH + (c + 1) * chunk, :] = act.astype(LOW)
        for b in range(blocks):
            lanes = slice(b * BLOCK, (b + 1) * BLOCK)
            agg = tn(adj[row, b], pad[b * BLOCK : b * BLOCK + WIDE, :])
            agg2[row, lanes, :] = (agg * cols[row, lanes, 2:3]).astype(LOW)
        if remote:
            @pl.when(row == 0)
            def _():
                gb.arrive(OWN, PASSED)
                gb.start(SIBLING)

    write(3, slope)
    write(4, hidden)
    write(5, agg2)
    if remote:
        gq.arrive(FIRST)
        gq.start(PASSED)
        gb.arrive(SIBLING)
        merge_rows(second_w, land_b)
        write(16, second_w)

    @pl.loop(0, rows)
    def _(row):
        for c in range(tokens // chunk):
            part = slice(c * chunk, (c + 1) * chunk)
            resid = x_ref[row, part, :].astype(F32) + nn(hidden[row, part, :], second_w[:, 0:width])
            resid = resid + nn(agg2[row, part, :], second_w[:, width : 2 * width])
            plain, scale = norm_parts(resid)
            unit[row, part, :] = plain.astype(LOW)
            rstd[row, part, :] = scale
            out = plain * gain_ref[0:1, :] + shift_ref[0:1, :]
            normed[row, part, :] = out
            low[row, part, :] = out.astype(LOW)
        if remote:
            @pl.when(row == 0)
            def _():
                for g in (go, gu):
                    g.arrive("along")
                    g.start(FIRST, OWN)
                begin(5)

    write(6, unit)
    write(7, rstd)
    write(8, normed)
    write(9, low)
    if remote:
        gq.arrive(OWN, PASSED)
        gq.start(SIBLING)
        for g in (go, gu):
            g.arrive(FIRST)
            g.start(PASSED)
        gq.arrive(SIBLING)
        merge_rows(third_w, land_q)
        write(17, third_w)

    @pl.loop(0, rows)
    def _(row):
        for c in range(tokens // chunk):
            part = slice(c * chunk, (c + 1) * chunk)
            out = nn(low[row, part, :], third_w[...]).astype(LOW)
            for k in range(3 * pairs):
                qkv[k, row, part, :] = out[:, k * BLOCK : (k + 1) * BLOCK]

    write(10, qkv)
    zeros = jnp.zeros((RADIUS, BLOCK), LOW)
    for ref in (keys, values):
        ref[pl.ds(0, RADIUS), :] = zeros
        ref[pl.ds(RADIUS + tokens, RADIUS), :] = zeros

    @pl.loop(0, rows * pairs)
    def _(turn):
        row, pair, slot = lax.div(turn, pairs), lax.rem(turn, pairs), lax.rem(turn, 2)
        if remote:
            @pl.when(turn == 1)
            def _():
                gd.arrive("along")
                gd.start(FIRST, OWN)

            @pl.when(turn == 4)
            def _():
                for g in (go, gu):
                    g.arrive(OWN, PASSED)
                    g.start(SIBLING)
                gd.arrive(FIRST)
                gd.start(PASSED)

            @pl.when(turn == 9)
            def _():
                gd.arrive(OWN, PASSED)
                gd.start(SIBLING)

        def probs_copy(t, s):
            return pltpu.make_async_copy(
                probs.at[s], outs[12].at[lax.div(t, pairs), lax.rem(t, pairs)], probs_sem.at[s]
            )

        @pl.when(turn >= 2)
        def _():
            probs_copy(turn - 2, slot).wait()

        keys[pl.ds(RADIUS, tokens), :] = qkv[pairs + pair, row]
        values[pl.ds(RADIUS, tokens), :] = qkv[2 * pairs + pair, row]
        for b in range(blocks):
            lanes = slice(b * BLOCK, (b + 1) * BLOCK)
            window = slice(b * BLOCK, b * BLOCK + SPAN)
            queries = pair_rows(qkv[pair, row, lanes, :] * 0.125)
            raw = nt(keys[window, :], queries)
            sides = []
            for h in range(2):
                bias = order_rate_ref[2 * pair + h] * order[row, b] - dist_rate_ref[2 * pair + h] * far[row, b]
                scores = raw[:, h * BLOCK : (h + 1) * BLOCK] + bias
                grown = jnp.exp(scores - jnp.max(scores, axis=0, keepdims=True))
                scale = 1.0 / jnp.sum(grown, axis=0, keepdims=True)
                sides.append((grown * scale).astype(LOW))
            both = jnp.concatenate(sides, axis=1)
            probs[slot, b] = both
            att[pair, row, lanes, :] = pair_pick(tn(both, values[window, :])).astype(LOW)
        probs_copy(turn, slot).start()

    last = rows * pairs
    for turn in (last - 2, last - 1):
        pltpu.make_async_copy(probs.at[turn % 2], outs[12].at[turn // pairs, turn % pairs], probs_sem.at[turn % 2]).wait()
    write(11, att)
    if remote:
        for g in (go, gu, gd):
            g.arrive(SIBLING)
        for g in groups:
            g.sent()
    for copy in writes.values():
        copy.wait()


def front(remote, depth, length, dist_rate, order_rate, near, count, point, x, edge_w, gains, shifts, weights, shards):
    rows, tokens, width = x.shape
    slots = near.shape[1]
    blocks, pairs = tokens // BLOCK, width // BLOCK
    smem, vmem, hbm = (pl.BlockSpec(memory_space=s) for s in (pltpu.SMEM, pltpu.VMEM, pl.ANY))
    each = lambda dtype, *shape: ((rows,) + shape, dtype)
    kept = [
        each(LOW, blocks, WIDE, BLOCK),
        each(F32, tokens, 8),
        each(LOW, tokens, width),
        each(LOW, tokens, width),
        each(LOW, tokens, width),
        each(LOW, tokens, width),
        each(LOW, tokens, width),
        each(F32, tokens, 1),
        each(F32, tokens, width),
        each(LOW, tokens, width),
        ((3 * pairs, rows, tokens, BLOCK), LOW),
        ((pairs, rows, tokens, BLOCK), LOW),
        each(LOW, pairs, blocks, SPAN, 2 * BLOCK),
        each(F32, blocks, SPAN, BLOCK),
        each(F32, blocks, SPAN, BLOCK),
        ((width, 2 * width), LOW),
        ((width, 2 * width), LOW),
        ((width, 3 * width), LOW),
    ]
    out_shape = [jax.ShapeDtypeStruct(*k) for k in kept]
    kept[12] = ((2, blocks, SPAN, 2 * BLOCK), LOW)
    scratch = [pltpu.VMEM(*k) for k in kept]
    scratch += [
        pltpu.VMEM((tokens + 2 * REACH, width), LOW),
        pltpu.VMEM((16, tokens + 2 * REACH), LOW),
        pltpu.VMEM((slots, BLOCK), jnp.int32),
        pltpu.VMEM((tokens + 2 * RADIUS, BLOCK), LOW),
        pltpu.VMEM((tokens + 2 * RADIUS, BLOCK), LOW),
        pltpu.SemaphoreType.DMA((18,)),
        pltpu.SemaphoreType.DMA((2,)),
        pltpu.SemaphoreType.DMA((8,)),
    ]
    more = {}
    if remote:
        blocked = lambda shape: (depth, 2, 2, 2) + shape
        out_shape += [jax.ShapeDtypeStruct(blocked(s.shape), LOW) for s in shards]
        share = weights[0].shape[0]
        scratch += [pltpu.VMEM(blocked((share, k * width)), LOW) for k in (2, 2, 3)]
        scratch += [pltpu.SemaphoreType.DMA((6, depth + 3))] * 2
        more = {"collective_id": 0, "has_side_effects": True}
    return pl.pallas_call(
        functools.partial(front_kernel, remote),
        in_specs=[smem] * 3 + [vmem] * 7 + [hbm] * (len(weights) + len(shards)),
        out_specs=[hbm] * len(out_shape),
        out_shape=out_shape,
        scratch_shapes=scratch,
        compiler_params=pltpu.CompilerParams(vmem_limit_bytes=VMEM, **more),
        name="front",
    )(length, dist_rate, order_rate, near, count, point, x, edge_w, gains, shifts, *weights, *shards)


def attention_back_kernel(
    q_ref, k_ref, v_ref, grad_ref, probs_ref, far_ref, order_ref,
    dq_ref, dk_ref, dv_ref, rate_ref,
    keys, values, grad_keys, grad_values,
):
    pad_rows(keys, k_ref[0, 0])
    pad_rows(values, v_ref[0, 0])
    grad_keys[...] = jnp.zeros_like(grad_keys)
    grad_values[...] = jnp.zeros_like(grad_values)
    tokens = q_ref.shape[2]
    sums = [jnp.zeros((8, BLOCK), F32)] * 4
    for b in range(tokens // BLOCK):
        lanes = slice(b * BLOCK, (b + 1) * BLOCK)
        window = slice(b * BLOCK, b * BLOCK + SPAN)
        queries = pair_rows(q_ref[0, 0, lanes, :] * 0.125)
        grads = pair_rows(grad_ref[0, lanes, :])
        probs_low = probs_ref[0, 0, b]
        back = nt(values[window, :], grads)
        dist = jnp.where(far_ref[0, b] < FAR, far_ref[0, b], 0.0)
        order = order_ref[0, b]
        sides = []
        for h in range(2):
            probs = probs_low[:, h * BLOCK : (h + 1) * BLOCK].astype(F32)
            part = back[:, h * BLOCK : (h + 1) * BLOCK]
            delta = jnp.sum(probs * part, axis=0, keepdims=True)
            scores = probs * (part - delta)
            sums[2 * h] = sums[2 * h] - fold(scores * dist)
            sums[2 * h + 1] = sums[2 * h + 1] + fold(scores * order)
            sides.append(scores.astype(LOW))
        scores_low = jnp.concatenate(sides, axis=1)
        grad_values[window, :] += nn(probs_low, grads)
        grad_keys[window, :] += nn(scores_low, queries)
        dq_ref[0, lanes, :] = (pair_pick(tn(scores_low, keys[window, :])) * 0.125).astype(LOW)
    dk_ref[0] = grad_keys[pl.ds(RADIUS, tokens), :].astype(LOW)
    dv_ref[0] = grad_values[pl.ds(RADIUS, tokens), :].astype(LOW)
    for k in range(4):
        rate_ref[0, 0, k] = sums[k]


def attention_backward(qkv, grad, probs, far, order):
    pairs, rows, tokens = qkv.shape[0] // 3, qkv.shape[1], qkv.shape[2]
    width = pairs * BLOCK
    blocks = tokens // BLOCK
    part = lambda k: pl.BlockSpec((1, 1, tokens, BLOCK), lambda r, p: (k * pairs + p, r, 0, 0))
    flat = pl.BlockSpec((1, tokens, BLOCK), lambda r, p: (r, 0, p))
    bias = pl.BlockSpec((1, blocks, SPAN, BLOCK), lambda r, p: (r, 0, 0, 0))
    grads = jax.ShapeDtypeStruct((rows, tokens, width), LOW)
    return pl.pallas_call(
        attention_back_kernel,
        grid=(rows, pairs),
        in_specs=[
            part(0),
            part(1),
            part(2),
            flat,
            pl.BlockSpec((1, 1, blocks, SPAN, 2 * BLOCK), lambda r, p: (r, p, 0, 0, 0)),
            bias,
            bias,
        ],
        out_specs=[flat] * 3 + [pl.BlockSpec((1, 1, 4, 8, BLOCK), lambda r, p: (r, p, 0, 0, 0))],
        out_shape=[grads] * 3 + [jax.ShapeDtypeStruct((rows, pairs, 4, 8, BLOCK), F32)],
        scratch_shapes=[pltpu.VMEM((tokens + 2 * RADIUS, BLOCK), LOW)] * 2
        + [pltpu.VMEM((tokens + 2 * RADIUS, BLOCK), F32)] * 2,
        compiler_params=params(2),
        name="attention_backward",
    )(qkv, qkv, qkv, grad, probs, far, order)


TILE = 256
PARTS = 6


def block_kernel(
    att_ref, normed_ref, cot_ref, out_w_ref, up_ref, down_ref, gain_ref, shift_ref,
    result_ref, grad_two_ref, grad_att_ref, grad_out_ref, grad_up_ref, grad_down_ref, norms_ref,
    act_all, up_all, second_all, down_all, attn_all, att_all, slope_tile,
):
    step = pl.program_id(0)
    width = normed_ref.shape[1]
    steps = act_all.shape[1] // TILE
    piece = act_all.shape[2]

    @pl.when(step == 0)
    def _():
        norms_ref[...] = jnp.zeros_like(norms_ref)

    @pl.when(step < steps)
    def _():
        at = pl.ds(pl.multiple_of(step * TILE, TILE), TILE)
        att = jnp.concatenate([att_ref[k] for k in range(att_ref.shape[0])], axis=1)
        att_all[at, :] = att
        resid = normed_ref[...] + nn(att, out_w_ref[...])
        unit_two, rstd_two = norm_parts(resid)
        gain_two, gain_three = gain_ref[1:2, :], gain_ref[2:3, :]
        normed = unit_two * gain_two + shift_ref[1:2, :]
        second = normed.astype(LOW)
        second_all[at, :] = second
        resid = normed
        for c in range(PARTS):
            cols = slice(c * piece, (c + 1) * piece)
            act, deriv = gelu_pair(nn(second, up_ref[:, cols]))
            slope_tile[:, cols] = deriv.astype(LOW)
            act = act.astype(LOW)
            act_all[c, at, :] = act
            resid = resid + nn(act, down_ref[cols, :])
        unit, rstd = norm_parts(resid)
        result_ref[...] = (unit * gain_three + shift_ref[2:3, :]).astype(LOW)
        cot = cot_ref[...].astype(F32)
        norms_ref[2] += fold(cot * unit)
        norms_ref[3] += fold(cot)
        grad = norm_back(cot, unit, rstd, gain_three)
        low = grad.astype(LOW)
        down_all[at, :] = low
        for c in range(PARTS):
            cols = slice(c * piece, (c + 1) * piece)
            up_low = (nt(low, down_ref[cols, :]) * slope_tile[:, cols].astype(F32)).astype(LOW)
            up_all[c, at, :] = up_low
            grad = grad + nt(up_low, up_ref[:, cols])
        norms_ref[0] += fold(grad * unit_two)
        norms_ref[1] += fold(grad)
        grad = norm_back(grad, unit_two, rstd_two, gain_two)
        grad_two_ref[...] = grad
        low = grad.astype(LOW)
        attn_all[at, :] = low
        grad_att_ref[...] = nt(low, out_w_ref[...]).astype(LOW)

    @pl.when(step >= steps)
    def _():
        c = step - steps
        grad_down_ref[...] = tn(act_all[c], down_all[...]).astype(LOW)
        grad_up_ref[...] = tn(second_all[...], up_all[c]).astype(LOW)
        cols = pl.ds(pl.multiple_of(c * BLOCK, BLOCK), BLOCK)
        grad_out_ref[...] = tn(att_all[:, cols], attn_all[...]).astype(LOW)


def block_both(att, normed, cot, out_w, up, down, gains, shifts):
    tokens, width = normed.shape
    wide = up.shape[1]
    steps = tokens // TILE
    piece = wide // PARTS
    tile = lambda cols: pl.BlockSpec((TILE, cols), lambda s: (jnp.minimum(s, steps - 1), 0))
    late = lambda s: jnp.maximum(s - steps, 0)
    return pl.pallas_call(
        block_kernel,
        grid=(steps + PARTS,),
        in_specs=[
            pl.BlockSpec((width // BLOCK, TILE, BLOCK), lambda s: (0, jnp.minimum(s, steps - 1), 0)), tile(width), tile(width),
            whole((width, width)), whole(up.shape), whole(down.shape), whole(gains.shape), whole(shifts.shape),
        ],
        out_specs=[
            tile(width), tile(width), tile(width),
            pl.BlockSpec((width // PARTS, width), lambda s: (late(s), 0)),
            pl.BlockSpec((width, piece), lambda s: (0, late(s))),
            pl.BlockSpec((piece, width), lambda s: (late(s), 0)),
            pl.BlockSpec((4, 8, width), lambda s: (0, 0, 0)),
        ],
        out_shape=[
            jax.ShapeDtypeStruct((tokens, width), LOW),
            jax.ShapeDtypeStruct((tokens, width), F32),
            jax.ShapeDtypeStruct((tokens, width), LOW),
            jax.ShapeDtypeStruct((width, width), LOW),
            jax.ShapeDtypeStruct(up.shape, LOW),
            jax.ShapeDtypeStruct(down.shape, LOW),
            jax.ShapeDtypeStruct((4, 8, width), F32),
        ],
        scratch_shapes=[
            pltpu.VMEM((PARTS, tokens, piece), LOW),
            pltpu.VMEM((PARTS, tokens, piece), LOW),
            pltpu.VMEM((tokens, width), LOW),
            pltpu.VMEM((tokens, width), LOW),
            pltpu.VMEM((tokens, width), LOW),
            pltpu.VMEM((tokens, width), LOW),
            pltpu.VMEM((TILE, wide), LOW),
        ],
        compiler_params=params(1),
        name="block_both",
    )(att, normed, cot, out_w, up, down, gains, shifts)


def graph_back_kernel(
    dq_ref, dk_ref, dv_ref, low_ref, two_ref, unit_ref, rstd_ref, slope_ref, hidden_ref, agg1_ref,
    agg2_ref, x_ref, adj_ref, cols_ref, first_ref, second_ref, qkv_w_ref, gain_ref,
    input_grad_ref, grad_qkv_ref, grad_graph_ref, norms_ref, edge_ref,
    branch_all, pre_all, one_row, mean_row, back_row,
):
    step = pl.program_id(0)
    rows, tokens, width = dq_ref.shape
    blocks = tokens // BLOCK
    chunk = 2 * BLOCK
    chunks = tokens // chunk

    @pl.when(step == 0)
    def _():
        norms_ref[...] = jnp.zeros_like(norms_ref)
        edge_ref[...] = jnp.zeros_like(edge_ref)

    def spread():
        back_row[...] = jnp.zeros_like(back_row)
        for b in range(blocks):
            back_row[b * BLOCK : b * BLOCK + WIDE, :] += nn(adj_ref[0, b], mean_row[b * BLOCK : (b + 1) * BLOCK, :])

    @pl.when(step < rows)
    def _():
        base = step * tokens
        for c in range(chunks):
            part = slice(c * chunk, (c + 1) * chunk)
            grad = two_ref[0, part, :]
            for k, ref in enumerate((dq_ref, dk_ref, dv_ref)):
                grad = grad + nt(ref[step, part, :], qkv_w_ref[:, k * width : (k + 1) * width])
            unit = unit_ref[0, part, :].astype(F32)
            norms_ref[0] += fold(grad * unit)
            norms_ref[1] += fold(grad)
            grad = norm_back(grad, unit, rstd_ref[0, part, :], gain_ref[0:1, :])
            one_row[part, :] = grad
            low = grad.astype(LOW)
            branch_all[pl.ds(pl.multiple_of(base + c * chunk, chunk), chunk), :] = low
            mean_row[part, :] = (nt(low, second_ref[:, width : 2 * width]) * cols_ref[0, part, 2:3]).astype(LOW)
        spread()
        for c in range(chunks):
            part = slice(c * chunk, (c + 1) * chunk)
            at = pl.ds(pl.multiple_of(base + c * chunk, chunk), chunk)
            grad = back_row[REACH + c * chunk : REACH + (c + 1) * chunk, :]
            grad = grad + nt(branch_all[at, :], second_ref[:, 0:width])
            grad = grad * slope_ref[0, part, :].astype(F32)
            edge_ref[0] += fold(grad * cols_ref[0, part, 0:1])
            edge_ref[1] += fold(grad * cols_ref[0, part, 1:2])
            low = grad.astype(LOW)
            pre_all[at, :] = low
            mean_row[part, :] = (nt(low, first_ref[:, width : 2 * width]) * cols_ref[0, part, 2:3]).astype(LOW)
        spread()
        for c in range(chunks):
            part = slice(c * chunk, (c + 1) * chunk)
            at = pl.ds(pl.multiple_of(base + c * chunk, chunk), chunk)
            grad = one_row[part, :] + back_row[REACH + c * chunk : REACH + (c + 1) * chunk, :]
            input_grad_ref[0, part, :] = grad + nt(pre_all[at, :], first_ref[:, 0:width])

    flat = lambda ref: ref[...].reshape(rows * tokens, width)
    for k, (left, right) in enumerate(
        ((low_ref, dq_ref), (low_ref, dk_ref), (low_ref, dv_ref))
    ):
        @pl.when(step == rows + k)
        def _(left=left, right=right):
            grad_qkv_ref[...] = tn(flat(left), flat(right)).astype(LOW)

    for k, (left, right) in enumerate(
        ((x_ref, pre_all), (agg1_ref, pre_all), (hidden_ref, branch_all), (agg2_ref, branch_all))
    ):
        @pl.when(step == rows + 3 + k)
        def _(left=left, right=right):
            grad_graph_ref[...] = tn(flat(left), right[...]).astype(LOW)


def graph_backward(dq, dk, dv, low, two, unit, rstd, slope, hidden, agg1, agg2, x, adj, cols, first_w, second_w, qkv_w, gains):
    rows, tokens, width = x.shape
    blocks = tokens // BLOCK
    per_row = lambda *shape: pl.BlockSpec(
        (1,) + shape, lambda s: (jnp.minimum(s, rows - 1),) + (0,) * len(shape)
    )
    full = whole((rows, tokens, width))
    return pl.pallas_call(
        graph_back_kernel,
        grid=(rows + 7,),
        in_specs=[
            full, full, full, full,
            per_row(tokens, width), per_row(tokens, width), per_row(tokens, 1), per_row(tokens, width),
            full, full, full, full,
            per_row(blocks, WIDE, BLOCK), per_row(tokens, 8),
            whole(first_w.shape), whole(second_w.shape), whole(qkv_w.shape), whole(gains.shape),
        ],
        out_specs=[
            per_row(tokens, width),
            pl.BlockSpec((width, width), lambda s: (0, jnp.clip(s - rows, 0, 2))),
            pl.BlockSpec((width, width), lambda s: (0, jnp.clip(s - rows - 3, 0, 3))),
            pl.BlockSpec((2, 8, width), lambda s: (0, 0, 0)),
            pl.BlockSpec((2, 8, width), lambda s: (0, 0, 0)),
        ],
        out_shape=[
            jax.ShapeDtypeStruct((rows, tokens, width), F32),
            jax.ShapeDtypeStruct((width, 3 * width), LOW),
            jax.ShapeDtypeStruct((width, 4 * width), LOW),
            jax.ShapeDtypeStruct((2, 8, width), F32),
            jax.ShapeDtypeStruct((2, 8, width), F32),
        ],
        scratch_shapes=[
            pltpu.VMEM((rows * tokens, width), LOW),
            pltpu.VMEM((rows * tokens, width), LOW),
            pltpu.VMEM((tokens, width), F32),
            pltpu.VMEM((tokens, width), LOW),
            pltpu.VMEM((tokens + 2 * REACH, width), F32),
        ],
        compiler_params=params(1),
        name="graph_backward",
    )(dq, dk, dv, low, two, unit, rstd, slope, hidden, agg1, agg2, x, adj, cols, first_w, second_w, qkv_w, gains)


def device_work(remote, depth, inputs, coords, neighbours, counts, doc_length, weights, shards,
                edge_proj, norm_gains, norm_shifts, distance_rate, order_rate, cotangent):
    rows, tokens, width = inputs.shape
    results = front(
        remote, depth, doc_length[:, 0], distance_rate, order_rate, neighbours, counts[:, None, :], coords, inputs,
        edge_proj, norm_gains, norm_shifts, weights, shards if remote else (),
    )
    (adj, cols, agg1, slope, hidden, agg2, unit, rstd, normed, low, qkv, att, probs, far, order, first_w, second_w, qkv_w) = results[:18]
    fulls = tuple(v.reshape(-1, v.shape[-1]) for v in results[18:]) if remote else shards
    out_w, up, down = fulls
    flat = lambda v: v.reshape(rows * tokens, width)
    tall = lambda v: v.reshape(rows, tokens, width)
    result, two, grad_att, grad_out, grad_up, grad_down, norms_late = block_both(
        att.reshape(-1, rows * tokens, BLOCK), flat(normed), flat(cotangent), out_w, up, down, norm_gains, norm_shifts
    )
    dq, dk, dv, rates = attention_backward(qkv, tall(grad_att), probs, far, order)
    input_grad, grad_qkv, grad_graph, norms_first, edge = graph_backward(
        dq, dk, dv, low, tall(two), unit, rstd, slope, hidden, agg1, agg2, inputs, adj, cols,
        first_w, second_w, qkv_w, norm_gains,
    )
    norms = jnp.concatenate([norms_first, norms_late], axis=0).sum(axis=1)
    rates = rates.sum(axis=(0, 3, 4)).reshape(-1, 2, 2)
    small = (edge.sum(axis=1), norms[0::2], norms[1::2], rates[:, :, 0].reshape(-1), rates[:, :, 1].reshape(-1))
    return tall(result), input_grad, grad_graph, grad_qkv, grad_out, grad_up, grad_down, small


def add_small(small, axes):
    edge, gains, shifts, rates, orders = small
    width = edge.shape[1]
    heads = rates.shape[0]
    line = jnp.concatenate([rates, orders, jnp.zeros((width - 2 * heads,), F32)])[None]
    total = lax.psum(jnp.concatenate([edge, gains, shifts, line], axis=0), axes)
    return total[0:2], total[2:5], total[5:8], total[8, :heads], total[8, heads : 2 * heads]


def local(
    sizes, inputs, coords, neighbours, counts, doc_length, self_one, near_one, self_two, near_two, edge_proj,
    qkv_proj, out_proj, up_proj, down_proj, norm_gains, norm_shifts, distance_rate, order_rate, cotangent,
):
    axes = ("wide", "narrow")
    width = inputs.shape[2]
    wide_size, narrow_size = sizes
    remote = wide_size % 4 == 0 and narrow_size == 2 and self_one.shape[0] % 8 == 0
    weights, shards = (self_one, near_one, self_two, near_two, qkv_proj), (out_proj, up_proj, down_proj)
    if not remote:
        gather = lambda v: lax.all_gather(v, axes, axis=0, tiled=True)
        weights, shards = tuple(map(gather, weights)), tuple(map(gather, shards))
    scatter = lambda v: lax.psum_scatter(v, axes, scatter_dimension=0, tiled=True)
    result, input_grad, grad_graph, grad_qkv, grad_out, grad_up, grad_down, small = device_work(
        remote, wide_size // 4, inputs, coords, neighbours, counts, doc_length, weights, shards,
        edge_proj, norm_gains, norm_shifts, distance_rate, order_rate, cotangent,
    )
    down_own = scatter(grad_down).astype(F32)
    up_own = scatter(jnp.concatenate([grad_up, grad_out], axis=1)).astype(F32)
    rest = scatter(jnp.concatenate([grad_graph, grad_qkv], axis=1)).astype(F32)
    edge, gains, shifts, rates, orders = add_small(small, axes)
    wide = up_proj.shape[1]
    return (
        result, input_grad,
        rest[:, :width], rest[:, width : 2 * width], rest[:, 2 * width : 3 * width], rest[:, 3 * width : 4 * width],
        edge,
        rest[:, 4 * width :], up_own[:, wide:], up_own[:, :wide], down_own,
        gains, shifts, rates, orders,
    )


def solution(mesh):
    axes = ("wide", "narrow")
    middle, last = P(None, axes, None), P(None, None, axes)
    count, weight, same = P(None, axes), P(axes, None), P()
    sizes = (mesh.shape["wide"], mesh.shape["narrow"])
    return jax.shard_map(
        functools.partial(local, sizes),
        mesh=mesh,
        in_specs=(middle, last, last, count, count)
        + (weight,) * 4
        + (same,)
        + (weight,) * 4
        + (same,) * 4
        + (middle,),
        out_specs=(middle, middle) + (weight,) * 4 + (same,) + (weight,) * 4 + (same,) * 4,
        check_vma=False,
    )
```

time: 735 us -> 577 us (0.79)
  waiting for transfers between devices: 392 us -> 198 us
  Pallas kernels: 242 us -> 285 us
    all_gather x4 -> x0, waiting for transfers between devices: 192 us -> none  [local(): gather = lambda v: lax.all_gather(v, axes, axis=0, tiled=True)]
    pallas_call x3 -> x2, Pallas kernels: 143 us -> 185 us  [the longest x1 106 us: front(): pl.pallas_call(functools.partial(front_kernel, remote), in_specs=[smem] *...]
  transfers between devices with their start and end apart: 7 -> 3, of which waited for: 5 -> 2; matrix products, arithmetic and copies ran while one was open for 4% -> 3% of each run, Pallas kernels for 22% -> 18%
where the time goes in v2:
time: 577 us; the launch traced here: 568 us
  Pallas kernels  285 us (49%)
  waiting for transfers between devices  198 us (34%)
  blocking collectives  44.6 us (8%)
  other arithmetic  14.3 us (2%)
  between operations  14 us (2%)
  local copies, waits for them, and re-layouts  11.8 us (2%)
    reduce_scatter x3, waiting for transfers between devices, local(): lax.psum_scatter(v, axes, scatter_dimension=0, tiled=True)  198 us
    pallas_call x1, Pallas kernels, front(): pl.pallas_call(functools.partial(front_kernel, remote), in_specs=[smem] *...  106 us
    pallas_call x1, Pallas kernels, block_both(): pl.pallas_call(block_kernel, grid=(steps + PARTS,), in_specs=[pl.BlockSpe...  79.6 us
    pallas_call x1, Pallas kernels, graph_backward(): pl.pallas_call(graph_back_kernel, grid=(rows + 7,), in_specs=[full, full,...  63.4 us
    psum x1, blocking collectives, add_small(): total = lax.psum(jnp.concatenate([edge, gains, shifts, line], axis=0), axes)  44.6 us
    pallas_call x1, Pallas kernels, attention_backward(): pl.pallas_call(attention_back_kernel, grid=(rows, pairs), in_specs=[part(...  36.4 us
  transfers between devices with their start and end apart: 3, of which 2 were waited for; matrix products, arithmetic and copies ran while one was open for 3% of the time, Pallas kernels for 18%

profile of v2, /device:TPU:0, one launch (start us, length us, event | category | flops | bytes accessed | tf_op | source)
XLA Modules:
  0.0 568.3 jit_solution(1395781939822562128)
XLA Ops:
  7.2 0.0 reduce-scatter.8.cloned.1.call-start
  7.2 1.3 broadcast_in_dim.9.refs_4_
  8.5 105.6 %front.1 = (bf16[2,6,256,128]{3,2,1,0:T(8,128)(2,1)}, f32[2,768,8]{2,1,0:T(8,128)}, bf16[2,768,768]{2,1,0:T(8,128)(2,1)}, bf16[2,768,768]{2,1,0:T(8,128)(2,1)}, ...) custom-call(s32[2]{0:T(128)} %bitcast.28, ...), custom_call_target="tpu_custom_call" | custom-call | tf_op jit(solution)/shard_map/front/pallas_call | solution.py:538
  114.2 79.6 %block_both.1 = (bf16[1536,768]{1,0:T(8,128)(2,1)}, f32[1536,768]{1,0:T(8,128)}, bf16[1536,768]{1,0:T(8,128)(2,1)}, bf16[768,768]{1,0:T(8,128)(2,1)}, bf16[768,3...) custom-call(bf16[6,1536,128]{2,1,0:T(8,128)(2,1)} %bitcast.24, f32[1536,768]{1,0:T(8,128)} %bitcast.20, ...), custom_call_target="tpu_custom_call" | custom-call | tf_op jit(solution)/shard_map/block_both/pallas_call | solution.py:691
  193.8 0.0 copy-start
  193.8 0.0 reduce-scatter.8.cloned.1.call-update
  193.8 0.0 reduce-scatter.6.cloned.1.call-start
  193.9 1.2 copy-done
  195.1 5.2 pad_maximum_fusion.1
  200.3 0.0 reduce-scatter.6.cloned.1.call-update
  200.3 0.0 reduce-scatter.4.cloned.1.call-start
  200.4 36.4 %attention_backward.1 = (bf16[2,768,768]{2,1,0:T(8,128)(2,1)}, bf16[2,768,768]{2,1,0:T(8,128)(2,1)}, bf16[2,768,768]{2,1,0:T(8,128)(2,1)}, f32[2,6,4,8,128]{4,3,2,1,0:T(8,128)}) custom-call(bf16[18,2,768,128]{3,2,1,0:T(8,128)(2,1)} %get-tuple-element.58.q_ref.k_ref.v_ref, bf16[18,2,768,128]{3,2,1,0:T(8,128)(2,1)} %get-tuple-element.58.q_ref.k_ref.v_ref, ...), custom_call_target="tpu_custom_call" | custom-call | tf_op jit(solution)/shard_map/attention_backward/pallas_call | solution.py:596
  236.7 63.4 %graph_backward.1 = (f32[2,768,768]{2,1,0:T(8,128)}, bf16[768,2304]{1,0:T(8,128)(2,1)}, bf16[768,3072]{1,0:T(8,128)(2,1)}, f32[2,8,768]{2,1,0:T(8,128)}, f32[2,8,768]{2,1,0:T(8,128)}) custom-call(bf16[2,768,768]{2,1,0:T(8,128)(2,1)} %get-tuple-element.63.dq_ref, bf16[2,768,768]{2,1,0:T(8,128)(2,1)} %get-tuple-element.64.dk_ref, ...), custom_call_target="tpu_custom_call" | custom-call | tf_op jit(solution)/shard_map/graph_backward/pallas_call | solution.py:808
  300.2 7.2 %pad_maximum_fusion = bf16[768,5376]{1,0:T(8,128)(2,1)} fusion(bf16[768,2304]{1,0:T(8,128)(2,1)} %get-tuple-element.81, bf16[768,3072]{1,0:T(8,128)(2,1)} %get-tuple-element.80), kind=kLoop, calls=%fused_computation | loop fusion | flops 16515072 | bytes 16515072 | tf_op jit(solution)/shard_map/concatenate | solution.py:898
  307.3 0.0 copy-start.2
  307.3 0.0 copy-start.4
  307.3 0.0 copy-start.1
  307.3 0.0 copy-start.3
  307.3 0.0 reduce-scatter.4.cloned.1.call-update
  307.4 0.9 copy-done.2
  308.2 0.0 copy-done.4
  308.3 0.0 copy-done.1
  308.3 0.1 reduce_sum.29
  308.4 0.1 copy.38
  308.5 0.1 copy.39
  308.6 0.1 reshape_squeeze.6
  308.7 0.1 copy.40
  308.8 0.1 reshape_squeeze.7
  308.9 0.1 pad_maximum_fusion.3
  309.0 0.0 copy-done.3
  309.0 44.6 %psum.7 = f32[9,768]{1,0:T(8,128)S(1)} all-reduce(f32[9,768]{1,0:T(8,128)S(1)} %pad_maximum_fusion.2), channel_id=1, replica_groups=mesh['wide'=16,'narrow'=2] {'wide','narrow'}, use_global_device_ids=true, to_apply=%region_4.0 | all-reduce | flops 6912 | bytes 55296 | tf_op jit(solution)/shard_map/psum | solution.py:875
  353.6 0.6 slice.70
  354.2 0.6 slice_bitcast_fusion
  354.8 0.6 fusion.1
  355.4 0.0 reduce-scatter.8.cloned.1.call-done
  355.4 1.6 convert_element_type.11
  357.0 65.0 %reduce-scatter.6.cloned.1.call-done = bf16[24,3840]{1,0:T(8,128)(2,1)} async-done(((bf16[768,3840]{1,0:T(8,128)(2,1)}), bf16[24,3840]{1,0:T(8,128)(2,1)}) %reduce-scatter.6.cloned.1.call-update) | async-done | bytes 184336 | tf_op jit(solution)/shard_map/reduce_scatter | solution.py:891
  422.1 1.6 slice.73
  423.7 1.4 slice.72
  425.1 133.3 %reduce-scatter.4.cloned.1.call-done = bf16[24,5376]{1,0:T(8,128)(2,1)} async-done(((bf16[768,5376]{1,0:T(8,128)(2,1)}), bf16[24,5376]{1,0:T(8,128)(2,1)}) %reduce-scatter.4.cloned.1.call-update) | async-done | bytes 258064 | tf_op jit(solution)/shard_map/reduce_scatter | solution.py:891
  558.5 1.5 fusion
  560.0 1.6 slice.71
  (8 shorter events, 0.1 us)
Async XLA Ops:
  7.2 348.2 %reduce-scatter.8.cloned.1.call-start = ((), (), s32[]{:S(2)}) async-start(), calls=%async_computation.5 | async-start | bytes 4866048 | tf_op jit(solution)/shard_map/reduce_scatter | solution.py:891
  193.8 1.3 copy-start
  193.8 228.3 %reduce-scatter.6.cloned.1.call-start = ((), (), s32[]{:S(2)}) async-start(), calls=%async_computation.4 | async-start | bytes 6082560 | tf_op jit(solution)/shard_map/reduce_scatter | solution.py:891
  200.3 358.1 %reduce-scatter.4.cloned.1.call-start = ((), (), s32[]{:S(2)}) async-start(), calls=%async_computation.3 | async-start | bytes 8515584 | tf_op jit(solution)/shard_map/reduce_scatter | solution.py:891
  307.3 0.9 copy-start.2
  307.3 0.9 copy-start.4
  307.3 1.0 copy-start.1
  307.3 1.7 copy-start.3
Sparse Core Ops, SparseCore 0:
  193.9 109.7 reduce-scatter.7
  310.3 111.7 reduce-scatter.5
  429.0 129.4 reduce-scatter.3
